TPU v7x, 32 devices: a whole 2x2x4 slice. The times are simulated.
32 devices in a mesh: seq: 8 (over z, x), dp: 4 (over y, core).
Axes of the slice: x: 2, y: 2, z: 4, core: 2. Of those that a mesh axis runs over, the one named last changes fastest.
Arguments:
- inputs: bfloat16 [8, 1024, 1024], P('dp', 'seq'), may hold values from -6 to 6
- cotangent: bfloat16 [8, 1024, 1024], P('dp', 'seq'), may hold values from -6 to 6
- attn_gain: bfloat16 [1024], P('seq'), may hold values from 0.099609375 to 1.8984375
- w_query: bfloat16 [1024, 512], P('seq'), may hold values from -0.1875 to 0.1875
- w_key: bfloat16 [1024, 512], P('seq'), may hold values from -0.1875 to 0.1875
- w_value: bfloat16 [1024, 1024], P('seq'), may hold values from -0.1875 to 0.1875
- w_gate: bfloat16 [1024, 1024], P('seq'), may hold values from -0.1875 to 0.1875
- w_rank_in: bfloat16 [1024, 16], P('seq'), may hold values from -0.1875 to 0.1875
- w_rank_out: bfloat16 [16, 512], P('seq'), may hold values from -1.5 to 1.5
- rank_bias: bfloat16 [512], P('seq'), may hold values from 1 to 7
- out_gain: bfloat16 [256], P('seq'), may hold values from 0.099609375 to 1.8984375
- w_out: bfloat16 [1024, 1024], P('seq'), may hold values from -0.375 to 0.375
- mlp_gain: bfloat16 [1024], P('seq'), may hold values from 0.099609375 to 1.8984375
- w_gate_ff: bfloat16 [1024, 2816], P('seq'), may hold values from -0.1875 to 0.1875
- w_up: bfloat16 [1024, 2816], P('seq'), may hold values from -0.1875 to 0.1875
- w_down: bfloat16 [2816, 1024], P('seq'), may hold values from -0.21875 to 0.21875
Outputs:
- output: bfloat16 [8, 1024, 1024], P('dp', 'seq')
- input_grad: bfloat16 [8, 1024, 1024], P('dp', 'seq')
- grad_attn_gain: float32 [1024], P('seq')
- grad_w_query: float32 [1024, 512], P('seq')
- grad_w_key: float32 [1024, 512], P('seq')
- grad_w_value: float32 [1024, 1024], P('seq')
- grad_w_gate: float32 [1024, 1024], P('seq')
- grad_w_rank_in: float32 [1024, 16], P('seq')
- grad_w_rank_out: float32 [16, 512], P('seq')
- grad_rank_bias: float32 [512], P('seq')
- grad_out_gain: float32 [256], P('seq')
- grad_w_out: float32 [1024, 1024], P('seq')
- grad_mlp_gain: float32 [1024], P('seq')
- grad_w_gate_ff: float32 [1024, 2816], P('seq')
- grad_w_up: float32 [1024, 2816], P('seq')
- grad_w_down: float32 [2816, 1024], P('seq')
All inputs are finite; a program needn't handle non-finite values.
Results may differ from a plain program's by a relative error of at most 0.03.
Values may be sent and summed in bfloat16 or wider, within the bound.
A program may use at most 192 MiB of HBM per device.

v0:
```python
import jax
import jax.numpy as jnp
from jax import lax
from jax.sharding import PartitionSpec as P

HEADS = 4
KH = 128
VH = 256
BLOCK = 64


EPS = 1e-06
HIGH = lax.Precision.HIGHEST


def entering(x, axis, combine, identity):
    count, position = (lax.axis_size(axis), lax.axis_index(axis))
    everything = jax.tree.map(
        lambda part, kind: lax.all_gather(part.astype(kind), axis), x, (jnp.bfloat16, jnp.bfloat16)
    )
    start = jax.tree.map(
        lambda part, zero: jnp.broadcast_to(jnp.asarray(zero, part.dtype), part.shape), x, identity
    )

    def lap(k, before):
        reached = k < position
        new = combine(
            before, jax.tree.map(lambda part, own: part[k].astype(own.dtype), everything, x)
        )
        return jax.tree.map(lambda a, b: jnp.where(reached, a, b), new, before)

    return lax.fori_loop(0, count, lap, start)


def entering_2(x, axis, join, neutral):
    count = lax.axis_size(axis)
    place = lax.axis_index(axis)
    ahead = count - 1 - place
    gathered = jax.tree.map(
        lambda a, kind: lax.all_gather(a.astype(kind), axis),
        x,
        jax.tree.map(lambda a: jnp.bfloat16 if a.dtype == jnp.float32 else a.dtype, x),
    )
    state = jax.tree.map(lambda a, e: jnp.zeros_like(a) + jnp.asarray(e, a.dtype), x, neutral)

    def one(lap, state):
        source = count - 1 - lap
        return join(
            state,
            jax.tree.map(
                lambda a, own: lax.dynamic_index_in_dim(a, source, 0, False).astype(own.dtype),
                gathered,
                x,
            ),
        )

    return lax.fori_loop(0, ahead, one, state)


def matmul(left, right):
    return jnp.dot(left, right, preferred_element_type=jnp.float32)


def inner_rows(left, right):
    return lax.dot_general(
        left, right, (((0,), (0,)), ((), ())), preferred_element_type=jnp.float32
    )


def times_transposed(left, right):
    return lax.dot_general(
        left, right, (((1,), (1,)), ((), ())), preferred_element_type=jnp.float32
    )


def rms_scale(source):
    return lax.rsqrt(jnp.mean(source * source, axis=-1, keepdims=True) + EPS)


def head_scale(source):
    return lax.rsqrt(jnp.maximum(jnp.mean(source * source, axis=-1, keepdims=True), 1.0))


def norm_back(grad_unit, unit, scale):
    return scale * (grad_unit - unit * jnp.mean(grad_unit * unit, axis=-1, keepdims=True))


def head_norm_back(grad_unit, unit, scale):
    live = jnp.where(scale < 1.0, 1.0, 0.0)
    return scale * (grad_unit - live * unit * jnp.mean(grad_unit * unit, axis=-1, keepdims=True))


def compose(earlier, later):
    return (earlier[0] * later[0], later[0][..., None] * earlier[1] + later[1])


def block_step(memory, pieces):
    queries, key_rows, values, log_decay = pieces
    running = jnp.cumsum(log_decay, axis=2)
    length = running.shape[2]
    target = lax.broadcasted_iota(jnp.int32, (length, length), 0)
    source = lax.broadcasted_iota(jnp.int32, (length, length), 1)
    causal = jnp.where(target >= source, 1.0, 0.0).astype(jnp.float32)
    rising = queries * jnp.exp(running)
    falling = key_rows * jnp.exp(-running)
    scores = jnp.einsum("bhtk,bhsk->bhts", rising, falling, precision=HIGH) * causal
    within = jnp.einsum("bhts,bhsv->bhtv", scores, values, precision=HIGH)
    across = jnp.einsum("bhtk,bhkv->bhtv", rising, memory, precision=HIGH)
    ending = running[:, :, -1:, :]
    carried = jnp.exp(ending - running) * key_rows
    deposit = jnp.einsum("bhsk,bhsv->bhkv", carried, values, precision=HIGH)
    return (jnp.exp(ending[:, :, 0, :])[:, :, :, None] * memory + deposit, within + across)


def to_blocks(source, width):
    seqs, span = (source.shape[0], source.shape[1])
    blocked = source.reshape(seqs, span // BLOCK, BLOCK, HEADS, width)
    return blocked.transpose(1, 0, 3, 2, 4)


def span_attention(queries, key_rows, values, log_decay, memory_in):
    seqs, span = (queries.shape[0], queries.shape[1])
    pieces = (
        to_blocks(queries, KH),
        to_blocks(key_rows, KH),
        to_blocks(values, VH),
        to_blocks(log_decay, KH),
    )
    memory_out, blocks_out = lax.scan(jax.checkpoint(block_step), memory_in, pieces)
    return (blocks_out.transpose(1, 0, 3, 2, 4).reshape(seqs, span, HEADS * VH), memory_out)


def forward(whole, inputs):
    (
        attn_gain,
        w_query,
        w_key,
        w_value,
        w_gate,
        w_rank_in,
        w_rank_out,
        rank_bias,
        out_gain,
        w_out,
        mlp_gain,
        w_gate_ff,
        w_up,
        w_down,
    ) = whole
    seqs, span, width = inputs.shape
    count = seqs * span
    rows_in = inputs.astype(jnp.float32).reshape(count, width)
    scale_in = rms_scale(rows_in)
    unit_in = rows_in * scale_in
    normed_in = (unit_in * attn_gain.astype(jnp.float32)).astype(jnp.bfloat16)
    queries = matmul(normed_in, w_query).astype(jnp.bfloat16)
    key_rows = matmul(normed_in, w_key).astype(jnp.bfloat16)
    values = matmul(normed_in, w_value).astype(jnp.bfloat16)
    gate_out = matmul(normed_in, w_gate)
    rank_rows = matmul(normed_in, w_rank_in)
    logits = jnp.dot(rank_rows, w_rank_out.astype(jnp.float32), precision=HIGH) + rank_bias.astype(
        jnp.float32
    )
    log_decay = (jax.nn.log_sigmoid(logits) / 16.0).reshape(seqs, span, HEADS * KH)
    scaled_queries = (queries.astype(jnp.float32) * KH ** (-0.5)).reshape(seqs, span, HEADS * KH)
    key_float = key_rows.astype(jnp.float32).reshape(seqs, span, HEADS * KH)
    value_float = values.astype(jnp.float32).reshape(seqs, span, HEADS * VH)
    running = jnp.cumsum(log_decay.reshape(seqs, span, HEADS, KH), axis=1)
    ending = running[:, -1]
    weighted_keys = jnp.exp(ending[:, None] - running) * key_float.reshape(seqs, span, HEADS, KH)
    deposit = jnp.einsum(
        "snhk,snhv->shkv", weighted_keys, value_float.reshape(seqs, span, HEADS, VH), precision=HIGH
    )
    passing = jnp.exp(ending)
    arrived = entering(
        (passing, deposit), "seq", compose, (jnp.ones_like(passing), jnp.zeros_like(deposit))
    )
    memory_in = arrived[1]
    mixed, memory_out = span_attention(scaled_queries, key_float, value_float, log_decay, memory_in)
    mixed_heads = mixed.reshape(count, HEADS, VH)
    scale_heads = head_scale(mixed_heads)
    unit_heads = mixed_heads * scale_heads
    heads_normed = (unit_heads * out_gain.astype(jnp.float32)).reshape(count, HEADS * VH)
    gated = (heads_normed * jax.nn.silu(gate_out)).astype(jnp.bfloat16)
    middle = rows_in + matmul(gated, w_out)
    scale_mid = rms_scale(middle)
    unit_mid = middle * scale_mid
    normed_mid = (unit_mid * mlp_gain.astype(jnp.float32)).astype(jnp.bfloat16)
    gate_ff = matmul(normed_mid, w_gate_ff)
    up_rows = matmul(normed_mid, w_up)
    hidden = (jax.nn.silu(gate_ff) * up_rows).astype(jnp.bfloat16)
    output = (middle + matmul(hidden, w_down)).astype(jnp.bfloat16).reshape(seqs, span, width)
    return (
        unit_in,
        scale_in,
        normed_in,
        scaled_queries,
        key_float,
        value_float,
        log_decay,
        running,
        memory_in,
        gate_out,
        rank_rows,
        logits,
        unit_heads,
        scale_heads,
        gated,
        unit_mid,
        scale_mid,
        normed_mid,
        gate_ff,
        up_rows,
        hidden,
        output,
    )


def backward(whole, kept, cotangent):
    (
        attn_gain,
        w_query,
        w_key,
        w_value,
        w_gate,
        w_rank_in,
        w_rank_out,
        rank_bias,
        out_gain,
        w_out,
        mlp_gain,
        w_gate_ff,
        w_up,
        w_down,
    ) = whole
    (
        unit_in,
        scale_in,
        normed_in,
        scaled_queries,
        key_float,
        value_float,
        log_decay,
        running,
        memory_in,
        gate_out,
        rank_rows,
        logits,
        unit_heads,
        scale_heads,
        gated,
        unit_mid,
        scale_mid,
        normed_mid,
        gate_ff,
        up_rows,
        hidden,
        output,
    ) = kept
    seqs, span, width = cotangent.shape
    count = seqs * span
    grad_rows = cotangent.reshape(count, width)
    grad_down = inner_rows(hidden, grad_rows)
    grad_hidden = times_transposed(grad_rows, w_down)
    sig_ff = jax.nn.sigmoid(gate_ff)
    slope_ff = sig_ff * (1.0 + gate_ff * (1.0 - sig_ff))
    grad_gate_ff = (grad_hidden * up_rows * slope_ff).astype(jnp.bfloat16)
    grad_up_rows = (grad_hidden * gate_ff * sig_ff).astype(jnp.bfloat16)
    grad_gate_ff_w = inner_rows(normed_mid, grad_gate_ff)
    grad_up_w = inner_rows(normed_mid, grad_up_rows)
    grad_normed_mid = times_transposed(grad_gate_ff, w_gate_ff) + times_transposed(
        grad_up_rows, w_up
    )
    grad_mlp_gain = jnp.sum(grad_normed_mid * unit_mid, axis=0)
    grad_middle = grad_rows.astype(jnp.float32) + norm_back(
        grad_normed_mid * mlp_gain.astype(jnp.float32), unit_mid, scale_mid
    )
    grad_branch = grad_middle.astype(jnp.bfloat16)
    grad_out_w = inner_rows(gated, grad_branch)
    grad_gated = times_transposed(grad_branch, w_out)
    sig_out = jax.nn.sigmoid(gate_out)
    slope_out = sig_out * (1.0 + gate_out * (1.0 - sig_out))
    gain_float = out_gain.astype(jnp.float32)
    heads_normed = (unit_heads * gain_float).reshape(count, HEADS * VH)
    grad_gate_out = (grad_gated * heads_normed * slope_out).astype(jnp.bfloat16)
    grad_heads = (grad_gated * gate_out * sig_out).reshape(count, HEADS, VH)
    grad_out_gain = jnp.sum(grad_heads * unit_heads, axis=(0, 1))
    grad_mixed = head_norm_back(grad_heads * gain_float, unit_heads, scale_heads).reshape(
        seqs, span, HEADS * VH
    )
    growth = jnp.exp(running)
    local_pull = jnp.einsum(
        "snhk,snhv->shkv",
        scaled_queries.reshape(seqs, span, HEADS, KH) * growth,
        grad_mixed.reshape(seqs, span, HEADS, VH),
        precision=HIGH,
    )
    passing = jnp.exp(running[:, -1])
    returned = entering_2(
        (passing, local_pull), "seq", compose, (jnp.ones_like(passing), jnp.zeros_like(local_pull))
    )

    def local_span(first, second, third, fourth):
        return span_attention(first, second, third, fourth, memory_in)

    unused, pullback = jax.vjp(local_span, scaled_queries, key_float, value_float, log_decay)
    grad_scaled, grad_key_float, grad_value_float, grad_decay = pullback((grad_mixed, returned[1]))
    grad_queries = (grad_scaled.reshape(count, HEADS * KH) * KH ** (-0.5)).astype(jnp.bfloat16)
    grad_keys = grad_key_float.reshape(count, HEADS * KH).astype(jnp.bfloat16)
    grad_values = grad_value_float.reshape(count, HEADS * VH).astype(jnp.bfloat16)
    grad_logits = grad_decay.reshape(count, HEADS * KH) * jax.nn.sigmoid(-logits) / 16.0
    grad_bias = jnp.sum(grad_logits, axis=0)
    grad_rank_out = jnp.einsum("rq,rk->qk", rank_rows, grad_logits, precision=HIGH)
    grad_rank_rows = jnp.einsum(
        "rk,qk->rq", grad_logits, w_rank_out.astype(jnp.float32), precision=HIGH
    )
    grad_rank_in = jnp.einsum(
        "rd,rq->dq", normed_in.astype(jnp.float32), grad_rank_rows, precision=HIGH
    )
    grad_query_w = inner_rows(normed_in, grad_queries)
    grad_key_w = inner_rows(normed_in, grad_keys)
    grad_value_w = inner_rows(normed_in, grad_values)
    grad_gate_w = inner_rows(normed_in, grad_gate_out)
    grad_normed_in = times_transposed(grad_queries, w_query) + times_transposed(grad_keys, w_key)
    grad_normed_in = (
        grad_normed_in
        + times_transposed(grad_values, w_value)
        + times_transposed(grad_gate_out, w_gate)
    )
    grad_normed_in = grad_normed_in + jnp.einsum(
        "rq,dq->rd", grad_rank_rows, w_rank_in.astype(jnp.float32), precision=HIGH
    )
    grad_attn_gain = jnp.sum(grad_normed_in * unit_in, axis=0)
    input_grad = grad_middle + norm_back(
        grad_normed_in * attn_gain.astype(jnp.float32), unit_in, scale_in
    )
    grads = (
        grad_attn_gain,
        grad_query_w,
        grad_key_w,
        grad_value_w,
        grad_gate_w,
        grad_rank_in,
        grad_rank_out,
        grad_bias,
        grad_out_gain,
        grad_out_w,
        grad_mlp_gain,
        grad_gate_ff_w,
        grad_up_w,
        grad_down,
    )
    return (grads, input_grad.astype(jnp.bfloat16).reshape(seqs, span, width))


def body(
    inputs,
    cotangent,
    attn_gain,
    w_query,
    w_key,
    w_value,
    w_gate,
    w_rank_in,
    w_rank_out,
    rank_bias,
    out_gain,
    w_out,
    mlp_gain,
    w_gate_ff,
    w_up,
    w_down,
):
    whole = (
        lax.all_gather(attn_gain, "seq", axis=0, tiled=True),
        lax.all_gather(w_query, "seq", axis=0, tiled=True),
        lax.all_gather(w_key, "seq", axis=0, tiled=True),
        lax.all_gather(w_value, "seq", axis=0, tiled=True),
        lax.all_gather(w_gate, "seq", axis=0, tiled=True),
        lax.all_gather(w_rank_in, "seq", axis=0, tiled=True),
        lax.all_gather(w_rank_out, "seq", axis=0, tiled=True),
        lax.all_gather(rank_bias, "seq", axis=0, tiled=True),
        lax.all_gather(out_gain, "seq", axis=0, tiled=True),
        lax.all_gather(w_out, "seq", axis=0, tiled=True),
        lax.all_gather(mlp_gain, "seq", axis=0, tiled=True),
        lax.all_gather(w_gate_ff, "seq", axis=0, tiled=True),
        lax.all_gather(w_up, "seq", axis=0, tiled=True),
        lax.all_gather(w_down, "seq", axis=0, tiled=True),
    )
    kept = forward(whole, inputs)
    output = kept[-1]
    whole = (
        lax.all_gather(attn_gain, "seq", axis=0, tiled=True),
        lax.all_gather(w_query, "seq", axis=0, tiled=True),
        lax.all_gather(w_key, "seq", axis=0, tiled=True),
        lax.all_gather(w_value, "seq", axis=0, tiled=True),
        lax.all_gather(w_gate, "seq", axis=0, tiled=True),
        lax.all_gather(w_rank_in, "seq", axis=0, tiled=True),
        lax.all_gather(w_rank_out, "seq", axis=0, tiled=True),
        lax.all_gather(rank_bias, "seq", axis=0, tiled=True),
        lax.all_gather(out_gain, "seq", axis=0, tiled=True),
        lax.all_gather(w_out, "seq", axis=0, tiled=True),
        lax.all_gather(mlp_gain, "seq", axis=0, tiled=True),
        lax.all_gather(w_gate_ff, "seq", axis=0, tiled=True),
        lax.all_gather(w_up, "seq", axis=0, tiled=True),
        lax.all_gather(w_down, "seq", axis=0, tiled=True),
    )
    kept = forward(whole, inputs)
    grads, input_grad = backward(whole, kept, cotangent)
    owned = (
        lax.psum_scatter(
            grads[0].astype(jnp.bfloat16), "seq", scatter_dimension=0, tiled=True
        ).astype(jnp.float32),
        lax.psum_scatter(
            grads[1].astype(jnp.bfloat16), "seq", scatter_dimension=0, tiled=True
        ).astype(jnp.float32),
        lax.psum_scatter(
            grads[2].astype(jnp.bfloat16), "seq", scatter_dimension=0, tiled=True
        ).astype(jnp.float32),
        lax.psum_scatter(
            grads[3].astype(jnp.bfloat16), "seq", scatter_dimension=0, tiled=True
        ).astype(jnp.float32),
        lax.psum_scatter(
            grads[4].astype(jnp.bfloat16), "seq", scatter_dimension=0, tiled=True
        ).astype(jnp.float32),
        lax.psum_scatter(
            grads[5].astype(jnp.bfloat16), "seq", scatter_dimension=0, tiled=True
        ).astype(jnp.float32),
        lax.psum_scatter(
            grads[6].astype(jnp.bfloat16), "seq", scatter_dimension=0, tiled=True
        ).astype(jnp.float32),
        lax.psum_scatter(
            grads[7].astype(jnp.bfloat16), "seq", scatter_dimension=0, tiled=True
        ).astype(jnp.float32),
        lax.psum_scatter(
            grads[8].astype(jnp.bfloat16), "seq", scatter_dimension=0, tiled=True
        ).astype(jnp.float32),
        lax.psum_scatter(
            grads[9].astype(jnp.bfloat16), "seq", scatter_dimension=0, tiled=True
        ).astype(jnp.float32),
        lax.psum_scatter(
            grads[10].astype(jnp.bfloat16), "seq", scatter_dimension=0, tiled=True
        ).astype(jnp.float32),
        lax.psum_scatter(
            grads[11].astype(jnp.bfloat16), "seq", scatter_dimension=0, tiled=True
        ).astype(jnp.float32),
        lax.psum_scatter(
            grads[12].astype(jnp.bfloat16), "seq", scatter_dimension=0, tiled=True
        ).astype(jnp.float32),
        lax.psum_scatter(
            grads[13].astype(jnp.bfloat16), "seq", scatter_dimension=0, tiled=True
        ).astype(jnp.float32),
    )
    summed = (
        lax.psum(owned[0].astype(jnp.bfloat16), "dp").astype(jnp.float32),
        lax.psum(owned[1].astype(jnp.bfloat16), "dp").astype(jnp.float32),
        lax.psum(owned[2].astype(jnp.bfloat16), "dp").astype(jnp.float32),
        lax.psum(owned[3].astype(jnp.bfloat16), "dp").astype(jnp.float32),
        lax.psum(owned[4].astype(jnp.bfloat16), "dp").astype(jnp.float32),
        lax.psum(owned[5].astype(jnp.bfloat16), "dp").astype(jnp.float32),
        lax.psum(owned[6].astype(jnp.bfloat16), "dp").astype(jnp.float32),
        lax.psum(owned[7].astype(jnp.bfloat16), "dp").astype(jnp.float32),
        lax.psum(owned[8].astype(jnp.bfloat16), "dp").astype(jnp.float32),
        lax.psum(owned[9].astype(jnp.bfloat16), "dp").astype(jnp.float32),
        lax.psum(owned[10].astype(jnp.bfloat16), "dp").astype(jnp.float32),
        lax.psum(owned[11].astype(jnp.bfloat16), "dp").astype(jnp.float32),
        lax.psum(owned[12].astype(jnp.bfloat16), "dp").astype(jnp.float32),
        lax.psum(owned[13].astype(jnp.bfloat16), "dp").astype(jnp.float32),
    )
    return (
        output,
        input_grad,
        summed[0],
        summed[1],
        summed[2],
        summed[3],
        summed[4],
        summed[5],
        summed[6],
        summed[7],
        summed[8],
        summed[9],
        summed[10],
        summed[11],
        summed[12],
        summed[13],
    )


def solution(mesh):
    placed = (
        P("dp", "seq", None),
        P("dp", "seq", None),
        P("seq"),
        P("seq", None),
        P("seq", None),
        P("seq", None),
        P("seq", None),
        P("seq", None),
        P("seq", None),
        P("seq"),
        P("seq"),
        P("seq", None),
        P("seq"),
        P("seq", None),
        P("seq", None),
        P("seq", None),
    )
    return jax.shard_map(
        body,
        mesh=mesh,
        in_specs=placed,
        out_specs=(
            P("dp", "seq", None),
            P("dp", "seq", None),
            P("seq"),
            P("seq", None),
            P("seq", None),
            P("seq", None),
            P("seq", None),
            P("seq", None),
            P("seq", None),
            P("seq"),
            P("seq"),
            P("seq", None),
            P("seq"),
            P("seq", None),
            P("seq", None),
            P("seq", None),
        ),
        check_vma=False,
    )
```

profile of v0, /device:TPU:0, one launch (start us, length us, event | category | flops | bytes accessed | tf_op | source)
XLA Modules:
  0.0 1537.7 jit_solution(2032571927449125772)
XLA Ops:
  13.8 23.2 %all-reduce.9 = (bf16[512]{0:T(512)(128)(2,1)S(1)}, bf16[256]{0:T(256)(128)(2,1)S(1)}) all-reduce(bf16[512]{0:T(512)(128)(2,1)S(1)} %dynamic-update-slice, bf16[256]{0:T(256)(128)(2,1)S(1)} %dynamic-update-slice.1), channel_id=1, replica_groups=mesh['seq'=8,'dp'=4] {'seq'}, use_global_device_ids=true, to_apply=%add.1 | all-reduce | flops 768 | bytes 3072
  37.0 16.4 %all-gather.3 = bf16[8,1,128]{2,1,0:T(2,128)(2,1)S(1)} all-gather(bf16[1,1,128]{2,1,0:T(2,128)(2,1)} %bitcast.451), channel_id=1, replica_groups=mesh['seq'=8,'dp'=4] {'seq'}, dimensions={0}, use_global_device_ids=true | all-gather | bytes 2304 | tf_op jit(solution)/shard_map/all_gather | solution.py:375
  53.4 26.3 %all-gather.4 = bf16[8,2,512]{2,1,0:T(2,128)(2,1)S(1)} all-gather(bf16[1,2,512]{2,1,0:T(2,128)(2,1)} %bitcast.450), channel_id=1, replica_groups=mesh['seq'=8,'dp'=4] {'seq'}, dimensions={0}, use_global_device_ids=true | all-gather | bytes 18432 | tf_op jit(solution)/shard_map/all_gather | solution.py:381
  79.8 26.3 %all_gather.39 = bf16[1024,16]{0,1:T(8,128)(2,1)S(1)} all-gather(bf16[128,16]{0,1:T(8,128)(2,1)} %param.33), channel_id=1, replica_groups=mesh['seq'=8,'dp'=4] {'seq'}, dimensions={0}, use_global_device_ids=true | all-gather | bytes 36864 | tf_op jit(solution)/shard_map/all_gather | solution.py:380
  118.2 26.5 %all-gather.19.cloned.1.call-done = bf16[1024,1024]{1,0:T(8,128)(2,1)} async-done(((bf16[128,1024]{1,0:T(8,128)(2,1)}), bf16[1024,1024]{1,0:T(8,128)(2,1)}) %all-gather.19.cloned.1.call-update) | async-done | bytes 2097168 | tf_op jit(solution)/shard_map/all_gather | solution.py:378
  156.2 18.1 %all-gather.5 = bf16[8,1,128]{2,1,0:T(2,128)(2,1)S(1)} all-gather(bf16[1,1,128]{2,1,0:T(2,128)(2,1)S(1)} %bitcast.452), channel_id=1, replica_groups=mesh['seq'=8,'dp'=4] {'seq'}, dimensions={0}, use_global_device_ids=true | all-gather | bytes 2304 | tf_op jit(solution)/shard_map/all_gather | solution.py:385
  174.3 26.5 %all-gather = bf16[16,1,4,128]{3,2,1,0:T(4,128)(2,1)S(1)} all-gather(bf16[2,1,4,128]{3,2,1,0:T(4,128)(2,1)S(1)} %get-tuple-element.712), channel_id=2, replica_groups=mesh['seq'=8,'dp'=4] {'seq'}, dimensions={0}, use_global_device_ids=true | all-gather | bytes 18432 | tf_op jit(solution)/shard_map/all_gather | solution.py:19
  233.1 18.4 %while.89 = (s32[]{:T(128)}, f32[2,4,128,256]{3,2,1,0:T(8,128)S(1)}, f32[2,2,4,64,256]{4,3,2,1,0:T(8,128)}, f32[2,2,4,64,128]{4,3,2,1,0:T(8,128)}, f32[2,2,4,64,...) while((s32[]{:T(128)}, ...), condition=%wide.region_6.7_spmd.clone, body=%wide.region_4.6_spmd.sunk.clone | while | flops 558866432 | bytes 17640600 | solution.py:129
  275.2 45.2 %all-gather.25.cloned.1.call-done = bf16[1024,1024]{1,0:T(8,128)(2,1)} async-done(((bf16[128,1024]{1,0:T(8,128)(2,1)}), bf16[1024,1024]{1,0:T(8,128)(2,1)}) %all-gather.25.cloned.1.call-update) | async-done | bytes 2097168 | tf_op jit(solution)/shard_map/all_gather | solution.py:384
  325.0 88.8 %all-gather.27.cloned.1.call-done = bf16[1024,2816]{1,0:T(8,128)(2,1)} async-done(((bf16[128,2816]{1,0:T(8,128)(2,1)}), bf16[1024,2816]{1,0:T(8,128)(2,1)}) %all-gather.27.cloned.1.call-update) | async-done | bytes 5767184 | tf_op jit(solution)/shard_map/all_gather | solution.py:386
  419.8 87.0 %all-gather.29.cloned.1.call-done = bf16[1024,2816]{1,0:T(8,128)(2,1)} async-done(((bf16[128,2816]{1,0:T(8,128)(2,1)}), bf16[1024,2816]{1,0:T(8,128)(2,1)}) %all-gather.29.cloned.1.call-update) | async-done | bytes 5767184 | tf_op jit(solution)/shard_map/all_gather | solution.py:387
  512.9 87.0 %all-gather.31.cloned.1.call-done = bf16[2816,1024]{1,0:T(8,128)(2,1)} async-done(((bf16[352,1024]{1,0:T(8,128)(2,1)}), bf16[2816,1024]{1,0:T(8,128)(2,1)}) %all-gather.31.cloned.1.call-update) | async-done | bytes 5767184 | tf_op jit(solution)/shard_map/all_gather | solution.py:388
  652.5 47.6 %all-gather.35.cloned.1.call-done = bf16[16,4,128,256]{3,2,1,0:T(8,128)(2,1)} async-done(((bf16[2,4,128,256]{3,2,1,0:T(8,128)(2,1)}), bf16[16,4,128,256]{3,2,1,0:T(8,128)(2,1)}) %all-gather.35.cloned.1.call-update) | async-done | bytes 4194320 | tf_op jit(solution)/shard_map/all_gather | solution.py:40
  711.5 38.7 %while.92 = (s32[]{:T(128)}, f32[2,4,128,256]{3,2,1,0:T(8,128)S(1)}, f32[2,2,4,64,128]{4,3,2,1,0:T(8,128)}, bf16[2,2,4,64,128]{4,3,2,1,0:T(8,128)(2,1)}, bf16[2,...) while((s32[]{:T(128)}, ...), condition=%wide.region_21.22_spmd.clone, body=%wide.region_16.21_spmd.sunk.clone | while | flops 1169301504 | bytes 49136072 | solution.py:129
  789.9 50.1 %reduce-scatter.20.cloned.1.call-done = bf16[128,1024]{1,0:T(8,128)(2,1)} async-done(((bf16[1024,1024]{1,0:T(8,128)(2,1)}), bf16[128,1024]{1,0:T(8,128)(2,1)}) %reduce-scatter.20.cloned.1.call-update) | async-done | bytes 262160 | tf_op jit(solution)/shard_map/reduce_scatter | solution.py:438
  839.9 65.9 %reduce-scatter.12.cloned.1.call-done = bf16[128,512]{1,0:T(8,128)(2,1)} async-done(((bf16[1024,512]{1,0:T(8,128)(2,1)}), bf16[128,512]{1,0:T(8,128)(2,1)}) %reduce-scatter.12.cloned.1.call-update) | async-done | bytes 131088 | tf_op jit(solution)/shard_map/reduce_scatter | solution.py:414
  905.8 66.2 %reduce-scatter.14.cloned.1.call-done = bf16[128,512]{1,0:T(8,128)(2,1)} async-done(((bf16[1024,512]{1,0:T(8,128)(2,1)}), bf16[128,512]{1,0:T(8,128)(2,1)}) %reduce-scatter.14.cloned.1.call-update) | async-done | bytes 131088 | tf_op jit(solution)/shard_map/reduce_scatter | solution.py:417
  972.0 70.3 %reduce-scatter.16.cloned.1.call-done = bf16[128,1024]{1,0:T(8,128)(2,1)} async-done(((bf16[1024,1024]{1,0:T(8,128)(2,1)}), bf16[128,1024]{1,0:T(8,128)(2,1)}) %reduce-scatter.16.cloned.1.call-update) | async-done | bytes 262160 | tf_op jit(solution)/shard_map/reduce_scatter | solution.py:420
  1042.3 112.5 %reduce-scatter.22.cloned.1.call-done = bf16[128,2816]{1,0:T(8,128)(2,1)} async-done(((bf16[1024,2816]{1,0:T(8,128)(2,1)}), bf16[128,2816]{1,0:T(8,128)(2,1)}) %reduce-scatter.22.cloned.1.call-update) | async-done | bytes 720912 | tf_op jit(solution)/shard_map/reduce_scatter | solution.py:444
  1154.8 113.3 %reduce-scatter.24.cloned.1.call-done = bf16[128,2816]{1,0:T(8,128)(2,1)} async-done(((bf16[1024,2816]{1,0:T(8,128)(2,1)}), bf16[128,2816]{1,0:T(8,128)(2,1)}) %reduce-scatter.24.cloned.1.call-update) | async-done | bytes 720912 | tf_op jit(solution)/shard_map/reduce_scatter | solution.py:447
  1268.1 113.3 %reduce-scatter.26.cloned.1.call-done = bf16[352,1024]{1,0:T(8,128)(2,1)} async-done(((bf16[2816,1024]{1,0:T(8,128)(2,1)}), bf16[352,1024]{1,0:T(8,128)(2,1)}) %reduce-scatter.26.cloned.1.call-update) | async-done | bytes 720912 | tf_op jit(solution)/shard_map/reduce_scatter | solution.py:450
  1386.0 36.0 %all-reduce.8 = (bf16[1024]{0:T(1024)(128)(2,1)S(1)}, bf16[16,512]{1,0:T(8,128)(2,1)S(1)}, bf16[512]{0:T(512)(128)(2,1)S(1)}, bf16[256]{0:T(256)(128)(2,1)S(1)}, bf16[1024]{0:T(1024)(128)(2,1)S(1)}) all-reduce(bf16[1024]{0:T(1024)(128)(2,1)S(1)} %get-tuple-element.599, ...), channel_id=5, replica_groups=mesh['seq'=8,'dp'=4] {'seq'}, use_global_device_ids=true, to_apply=%region_24.25.clone | all-reduce | flops 11008 | bytes 44032
  1423.4 22.9 %reduce-scatter.28.cloned.1.call-done = bf16[128,16]{1,0:T(8,128)(2,1)} async-done(((bf16[1024,16]{1,0:T(8,128)(2,1)}), bf16[128,16]{1,0:T(8,128)(2,1)}) %reduce-scatter.28.cloned.1.call-update) | async-done | bytes 4112
  1456.2 62.8 %all-reduce.14.cloned.1.call-done = (bf16[128,512]{1,0:T(8,128)(2,1)}, bf16[128,512]{1,0:T(8,128)(2,1)}, bf16[128,1024]{1,0:T(8,128)(2,1)}, bf16[128,1024]{1,0:T...) async-done(((bf16[128,512]{1,0:T(8,128)(2,1)}, bf16[128,512]{1,0:T(8,128)(2,1)}, ...) | async-done | bytes 3211280 | tf_op jit(solution)/shard_map/psum | solution.py:456
  (430 shorter events, 315.5 us)
Async XLA Ops:
  7.2 104.3 %all-gather.21.cloned.1.call-start = ((), (), s32[]{:S(2)}) async-start(), calls=%async_computation.11 | async-start | bytes 1179648 | tf_op jit(solution)/shard_map/all_gather | solution.py:376
  7.9 105.5 %all-gather.17.cloned.1.call-start = ((), (), s32[]{:S(2)}) async-start(), calls=%async_computation.9 | async-start | bytes 1179648 | tf_op jit(solution)/shard_map/all_gather | solution.py:377
  8.7 136.0 %all-gather.19.cloned.1.call-start = ((), (), s32[]{:S(2)}) async-start(), calls=%async_computation.10 | async-start | bytes 2359296 | tf_op jit(solution)/shard_map/all_gather | solution.py:378
  9.4 211.8 %all-gather.33.cloned.1.call-start = ((), (), s32[]{:S(2)}) async-start(), calls=%async_computation.25 | async-start | bytes 4718592 | tf_op jit(solution)/shard_map/all_gather | solution.py:19
  79.8 30.6 %copy-start.54 = (bf16[16,512]{1,0:T(8,128)(2,1)}, bf16[16,512]{1,0:T(8,128)(2,1)S(1)}, u32[]{:S(2)}) copy-start(bf16[16,512]{1,0:T(8,128)(2,1)S(1)} %reshape.328) | copy-start | bytes 49156
  108.6 519.8 %copy-start.6 = (bf16[256,1024]{1,0:T(8,128)(2,1)}, bf16[256,1024]{1,0:T(8,128)(2,1)S(1)}, u32[]{:S(2)}) copy-start(bf16[256,1024]{1,0:T(8,128)(2,1)S(1)} %multiply_convert_fusion.7) | copy-start | bytes 1572868
  148.8 121.9 %all-gather.23.cloned.1.call-start = ((), (), s32[]{:S(2)}) async-start(), calls=%async_computation.12 | async-start | bytes 2359296 | tf_op jit(solution)/shard_map/all_gather | solution.py:379
  149.4 171.1 %all-gather.25.cloned.1.call-start = ((), (), s32[]{:S(2)}) async-start(), calls=%async_computation.13 | async-start | bytes 2359296 | tf_op jit(solution)/shard_map/all_gather | solution.py:384
  150.0 263.8 %all-gather.27.cloned.1.call-start = ((), (), s32[]{:S(2)}) async-start(), calls=%async_computation.14 | async-start | bytes 6488064 | tf_op jit(solution)/shard_map/all_gather | solution.py:386
  150.7 356.1 %all-gather.29.cloned.1.call-start = ((), (), s32[]{:S(2)}) async-start(), calls=%async_computation.15 | async-start | bytes 6488064 | tf_op jit(solution)/shard_map/all_gather | solution.py:387
  151.5 448.4 %all-gather.31.cloned.1.call-start = ((), (), s32[]{:S(2)}) async-start(), calls=%async_computation.16 | async-start | bytes 6488064 | tf_op jit(solution)/shard_map/all_gather | solution.py:388
  152.2 547.9 %all-gather.35.cloned.1.call-start = ((), (), s32[]{:S(2)}) async-start(), calls=%async_computation.26 | async-start | bytes 4718592 | tf_op jit(solution)/shard_map/all_gather | solution.py:40
  270.7 49.8 %copy-start.4 = (bf16[2,128,1024]{2,1,0:T(8,128)(2,1)S(1)}, bf16[2,128,1024]{2,1,0:T(8,128)(2,1)}, u32[]{:S(2)}) copy-start(bf16[2,128,1024]{2,1,0:T(8,128)(2,1)} %param.26) | copy-start | bytes 1572868
  628.3 161.5 %reduce-scatter.18.cloned.1.call-start = ((), (), s32[]{:S(2)}) async-start(), calls=%async_computation.20 | async-start | bytes 2359296 | tf_op jit(solution)/shard_map/reduce_scatter | solution.py:423
  631.6 208.3 %reduce-scatter.20.cloned.1.call-start = ((), (), s32[]{:S(2)}) async-start(), calls=%async_computation.21 | async-start | bytes 2359296 | tf_op jit(solution)/shard_map/reduce_scatter | solution.py:438
  649.9 255.9 %reduce-scatter.12.cloned.1.call-start = ((), (), s32[]{:S(2)}) async-start(), calls=%async_computation.17 | async-start | bytes 1179648 | tf_op jit(solution)/shard_map/reduce_scatter | solution.py:414
  754.1 217.9 %reduce-scatter.14.cloned.1.call-start = ((), (), s32[]{:S(2)}) async-start(), calls=%async_computation.18 | async-start | bytes 1179648 | tf_op jit(solution)/shard_map/reduce_scatter | solution.py:417
  755.9 286.4 %reduce-scatter.16.cloned.1.call-start = ((), (), s32[]{:S(2)}) async-start(), calls=%async_computation.19 | async-start | bytes 2359296 | tf_op jit(solution)/shard_map/reduce_scatter | solution.py:420
  758.8 396.0 %reduce-scatter.22.cloned.1.call-start = ((), (), s32[]{:S(2)}) async-start(), calls=%async_computation.22 | async-start | bytes 6488064 | tf_op jit(solution)/shard_map/reduce_scatter | solution.py:444
  763.0 505.0 %reduce-scatter.24.cloned.1.call-start = ((), (), s32[]{:S(2)}) async-start(), calls=%async_computation.23 | async-start | bytes 6488064 | tf_op jit(solution)/shard_map/reduce_scatter | solution.py:447
  768.6 612.8 %reduce-scatter.26.cloned.1.call-start = ((), (), s32[]{:S(2)}) async-start(), calls=%async_computation.24 | async-start | bytes 6488064 | tf_op jit(solution)/shard_map/reduce_scatter | solution.py:450
  774.3 672.0 %reduce-scatter.28.cloned.1.call-start = ((), (), s32[]{:S(2)}) async-start(), calls=%async_computation.27 | async-start | bytes 294912
  788.0 731.0 %all-reduce.14.cloned.1.call-start = ((), (), s32[]{:S(2)}) async-start(), calls=%async_computation.28 | async-start | bytes 6422528 | tf_op jit(solution)/shard_map/psum | solution.py:456
  1385.0 37.3 %copy-start.10 = (f32[256,1024]{1,0:T(8,128)S(1)}, f32[256,1024]{1,0:T(8,128)}, u32[]{:S(2)}) copy-start(f32[256,1024]{1,0:T(8,128)} %copy-done.9) | copy-start | bytes 3145732
  (70 other events, 194.4 us)
Sparse Core Ops, SparseCore 0:
  10.1 42.9 all-gather.20
  55.3 39.0 all-gather.16
  96.5 48.0 all-gather.18
  148.9 72.2 all-gather.32
  223.2 47.4 all-gather.22
  272.6 47.7 all-gather.24
  322.6 91.1 all-gather.26
  416.0 90.8 all-gather.28
  509.0 90.8 all-gather.30
  628.5 71.5 all-gather.34
  703.6 66.1 reduce-scatter.17
  773.2 66.7 reduce-scatter.19
  843.3 62.4 reduce-scatter.11
  909.5 62.4 reduce-scatter.13
  975.3 66.8 reduce-scatter.15
  1045.7 108.9 reduce-scatter.21
  1158.2 109.7 reduce-scatter.23
  1271.6 109.7 reduce-scatter.25
  1385.3 61.0 reduce-scatter.27
  1449.1 69.8 all-reduce.13
where the time goes:
time: 1550 us; the launch traced here: 1540 us
  waiting for transfers between devices  1090 us (70%)
  blocking collectives  179 us (12%)
  matrix products  123 us (8%)
  local copies, waits for them, and re-layouts  64.4 us (4%)
  other arithmetic  59.9 us (4%)
  between operations  19.4 us (1%)
    reduce_scatter x1, waiting for transfers between devices, body(): lax.psum_scatter(grads[12].astype(jnp.bfloat16), 'seq', scatter_dimension...  113 us
    reduce_scatter x1, waiting for transfers between devices, body(): lax.psum_scatter(grads[13].astype(jnp.bfloat16), 'seq', scatter_dimension...  113 us
    reduce_scatter x1, waiting for transfers between devices, body(): lax.psum_scatter(grads[11].astype(jnp.bfloat16), 'seq', scatter_dimension...  112 us
    all_gather x1, waiting for transfers between devices, body(): lax.all_gather(w_gate_ff, 'seq', axis=0, tiled=True)  88.8 us
    all_gather x1, waiting for transfers between devices, body(): lax.all_gather(w_up, 'seq', axis=0, tiled=True)  87 us
    all_gather x1, waiting for transfers between devices, body(): lax.all_gather(w_down, 'seq', axis=0, tiled=True)  87 us
    reduce_scatter x1, waiting for transfers between devices, body(): lax.psum_scatter(grads[3].astype(jnp.bfloat16), 'seq', scatter_dimension=...  70.3 us
    reduce_scatter x1, waiting for transfers between devices, body(): lax.psum_scatter(grads[2].astype(jnp.bfloat16), 'seq', scatter_dimension=...  66.2 us
  transfers between devices with their start and end apart: 20, of which 17 were waited for; matrix products, arithmetic and copies ran while one was open for 13% of the time, Pallas kernels for 0%

commit v1 on v0

--- a/solution.py
+++ b/solution.py
@@ -1,6 +1,10 @@
+import functools
+
 import jax
 import jax.numpy as jnp
 from jax import lax
+from jax.experimental import pallas as pl
+from jax.experimental.pallas import tpu as pltpu
 from jax.sharding import PartitionSpec as P
 
 HEADS = 4
@@ -13,48 +17,438 @@
 HIGH = lax.Precision.HIGHEST
 
 
-def entering(x, axis, combine, identity):
-    count, position = (lax.axis_size(axis), lax.axis_index(axis))
-    everything = jax.tree.map(
-        lambda part, kind: lax.all_gather(part.astype(kind), axis), x, (jnp.bfloat16, jnp.bfloat16)
-    )
-    start = jax.tree.map(
-        lambda part, zero: jnp.broadcast_to(jnp.asarray(zero, part.dtype), part.shape), x, identity
-    )
-
-    def lap(k, before):
-        reached = k < position
-        new = combine(
-            before, jax.tree.map(lambda part, own: part[k].astype(own.dtype), everything, x)
-        )
-        return jax.tree.map(lambda a, b: jnp.where(reached, a, b), new, before)
-
-    return lax.fori_loop(0, count, lap, start)
-
-
-def entering_2(x, axis, join, neutral):
-    count = lax.axis_size(axis)
-    place = lax.axis_index(axis)
-    ahead = count - 1 - place
-    gathered = jax.tree.map(
-        lambda a, kind: lax.all_gather(a.astype(kind), axis),
-        x,
-        jax.tree.map(lambda a: jnp.bfloat16 if a.dtype == jnp.float32 else a.dtype, x),
-    )
-    state = jax.tree.map(lambda a, e: jnp.zeros_like(a) + jnp.asarray(e, a.dtype), x, neutral)
-
-    def one(lap, state):
-        source = count - 1 - lap
-        return join(
-            state,
-            jax.tree.map(
-                lambda a, own: lax.dynamic_index_in_dim(a, source, 0, False).astype(own.dtype),
-                gathered,
-                x,
-            ),
-        )
-
-    return lax.fori_loop(0, ahead, one, state)
+MESH = pl.DeviceIdType.MESH
+ROWS = 16
+SMALL = 16
+
+
+def ring_place(index, n):
+    odd = index % 2
+    return (1 - odd) * (index // 2) + odd * (n - 1 - index // 2)
+
+
+def ring_index(place, n):
+    place = (place + 2 * n) % n
+    late = place // (n // 2)
+    return (1 - late) * 2 * place + late * (2 * (n - 1 - place) + 1)
+
+
+def greet(devices):
+    barrier = pltpu.get_barrier_semaphore()
+    for device in devices:
+        pl.semaphore_signal(barrier, inc=1, device_id=device, device_id_type=MESH)
+    pl.semaphore_wait(barrier, len(devices))
+
+
+def halves(width):
+    first = (width // 256) * 128
+    return ((0, first), (first, width - first))
+
+
+def gather_kernel(n, many, *refs):
+    shards, wholes = refs[:many], refs[many : 2 * many]
+    local_sem, ring_send, ring_recv, pair_send, pair_recv = refs[2 * many :]
+    me, replica = lax.axis_index("seq"), lax.axis_index("dp")
+    core = replica % 2
+    place = ring_place(me, n)
+    pair = (me, replica + 1 - 2 * core)
+    onward = [(ring_index(place + 1, n), replica), (ring_index(place - 1, n), replica)]
+    greet([*onward, pair])
+
+    def piece(a, way, half):
+        rows = shards[a].shape[0] // 2
+        start, size = halves(shards[a].shape[1])[way]
+        return (pl.ds(pl.multiple_of(half * rows, ROWS), rows), pl.ds(start, size))
+
+    def block(way, k):
+        return ring_index(place - k if way == 0 else place + k, n)
+
+    def own(a):
+        return pltpu.make_async_copy(shards[a], wholes[a].at[me], local_sem.at[a])
+
+    def ring(way, k, a, arriving):
+        where = piece(a, way, core)
+        here = wholes[a].at[(block(way, k + 1 if arriving else k), *where)]
+        return pltpu.make_async_remote_copy(
+            src_ref=shards[a].at[where] if k == 0 and not arriving else here,
+            dst_ref=here,
+            send_sem=ring_send.at[way, k, a],
+            recv_sem=ring_recv.at[way, k, a],
+            device_id=onward[way],
+            device_id_type=MESH,
+        )
+
+    def across(way, k, a, half):
+        here = wholes[a].at[(block(way, k + 1), *piece(a, way, half))]
+        return pltpu.make_async_remote_copy(
+            src_ref=here,
+            dst_ref=here,
+            send_sem=pair_send.at[way, k, a],
+            recv_sem=pair_recv.at[way, k, a],
+            device_id=pair,
+            device_id_type=MESH,
+        )
+
+    steps = [(k, a, way) for k in range(n - 1) for a in range(many) for way in range(2)]
+    for k, a, way in steps:
+        if k > 0:
+            ring(way, k - 1, a, True).wait_recv()
+        ring(way, k, a, False).start()
+        if k > 0:
+            across(way, k - 1, a, core).start()
+    for a in range(many):
+        own(a).start()
+    for a in range(many):
+        for way in range(2):
+            ring(way, n - 2, a, True).wait_recv()
+            across(way, n - 2, a, core).start()
+    for k, a, way in steps:
+        across(way, k, a, 1 - core).wait_recv()
+    for k, a, way in steps:
+        ring(way, k, a, False).wait_send()
+        across(way, k, a, core).wait_send()
+    for a in range(many):
+        own(a).wait()
+
+
+def gather_all(shards):
+    n, many = lax.axis_size("seq"), len(shards)
+    anywhere = pl.BlockSpec(memory_space=pl.ANY)
+    sems = pltpu.SemaphoreType.DMA((2, n - 1, many))
+    wholes = pl.pallas_call(
+        functools.partial(gather_kernel, n, many),
+        out_shape=[jax.ShapeDtypeStruct((n, *shard.shape), shard.dtype) for shard in shards],
+        in_specs=[anywhere] * many,
+        out_specs=[anywhere] * many,
+        scratch_shapes=[pltpu.SemaphoreType.DMA((many,)), sems, sems, sems, sems],
+        compiler_params=pltpu.CompilerParams(collective_id=0, has_side_effects=True),
+    )(*shards)
+    return [whole.reshape(-1, whole.shape[-1]) for whole in wholes]
+
+
+def reduce_kernel(n, many, joined, *refs):
+    grads, sums = refs[:many], refs[many : 2 * many]
+    own, other, first, second, fresh = (refs[(2 + i) * many : (3 + i) * many] for i in range(5))
+    (
+        local_sem,
+        pair_send,
+        pair_recv,
+        ring_send,
+        ring_recv,
+        peer_send,
+        peer_recv,
+        back_send,
+        back_recv,
+        out_sem,
+    ) = refs[7 * many :]
+    moving = (first, second)
+    me, replica = lax.axis_index("seq"), lax.axis_index("dp")
+    core = replica % 2
+    place = ring_place(me, n)
+    pair = (me, replica + 1 - 2 * core)
+    peer = (me, (replica + 2) % 4)
+    onward = [(ring_index(place + 1, n), replica), (ring_index(place - 1, n), replica)]
+    greet([*onward, pair, peer] if joined else [*onward, pair])
+
+    def rows_of(a, half):
+        rows = grads[a].shape[1] // 2
+        return pl.ds(pl.multiple_of(half * rows, ROWS), rows)
+
+    def columns(a, way):
+        start, size = halves(grads[a].shape[2])[way]
+        return pl.ds(start, size)
+
+    def block(way, k):
+        return ring_index(place - 1 - k if way == 0 else place + 1 + k, n)
+
+    def load(j, b, a):
+        return pltpu.make_async_copy(
+            grads[a].at[b, rows_of(a, core)], own[a].at[b], local_sem.at[j, a]
+        )
+
+    def across(j, b, a):
+        return pltpu.make_async_remote_copy(
+            src_ref=grads[a].at[b, rows_of(a, 1 - core)],
+            dst_ref=other[a].at[b],
+            send_sem=pair_send.at[j, a],
+            recv_sem=pair_recv.at[j, a],
+            device_id=pair,
+            device_id_type=MESH,
+        )
+
+    def ring(way, k, a):
+        source = own[a].at[block(way, 0), :, columns(a, way)] if k == 0 else moving[way][a].at[k - 1]
+        return pltpu.make_async_remote_copy(
+            src_ref=source,
+            dst_ref=moving[way][a].at[k],
+            send_sem=ring_send.at[way, k, a],
+            recv_sem=ring_recv.at[way, k, a],
+            device_id=onward[way],
+            device_id_type=MESH,
+        )
+
+    def trade(way, a):
+        return pltpu.make_async_remote_copy(
+            src_ref=own[a].at[me, :, columns(a, way)],
+            dst_ref=fresh[a].at[:, columns(a, way)],
+            send_sem=peer_send.at[way, a],
+            recv_sem=peer_recv.at[way, a],
+            device_id=peer,
+            device_id_type=MESH,
+        )
+
+    def put(a):
+        return pltpu.make_async_copy(own[a].at[me], sums[a].at[rows_of(a, core)], out_sem.at[a])
+
+    def back(a, half):
+        return pltpu.make_async_remote_copy(
+            src_ref=own[a].at[me],
+            dst_ref=sums[a].at[rows_of(a, half)],
+            send_sem=back_send.at[a],
+            recv_sem=back_recv.at[a],
+            device_id=pair,
+            device_id_type=MESH,
+        )
+
+    def sweep(a, act):
+        def turn(i, carry):
+            act(pl.ds(pl.multiple_of(i * ROWS, ROWS), ROWS))
+            return carry
+
+        lax.fori_loop(0, grads[a].shape[1] // 2 // ROWS, turn, 0)
+
+    order = []
+    for k in range(n // 2):
+        order.append(block(0, k))
+        if len(order) < n - 1:
+            order.append(block(1, k))
+    order = order[: n - 1] + [me]
+    for j, b in enumerate(order):
+        for a in range(many):
+            across(j, b, a).start()
+            load(j, b, a).start()
+
+    ready = set()
+
+    def need(j, a):
+        if (j, a) not in ready:
+            ready.add((j, a))
+            load(j, order[j], a).wait()
+            across(j, order[j], a).wait_recv()
+
+    def slot(way, k):
+        if k == n - 1:
+            return n - 1
+        return 2 * k + way if 2 * k + way < n - 1 and k < n // 2 else 2 * (n - 2 - k) + 1 - way
+
+    def add(way, k, a):
+        need(slot(way, k), a)
+        b, across_columns = block(way, k), columns(a, way)
+        if k == 0 or k == n - 1:
+            target, at = own[a], lambda rows: (b, rows, across_columns)
+        else:
+            target, at = moving[way][a], lambda rows: (k - 1, rows, slice(None))
+
+        def act(rows):
+            total = own[a][b, rows, across_columns].astype(jnp.float32)
+            total = total + other[a][b, rows, across_columns].astype(jnp.float32)
+            if k > 0:
+                total = total + moving[way][a][k - 1, rows, :].astype(jnp.float32)
+            target[at(rows)] = total.astype(jnp.bfloat16)
+
+        sweep(a, act)
+
+    for k in range(n):
+        for a in range(many):
+            for way in range(2):
+                if k > 0:
+                    ring(way, k - 1, a).wait_recv()
+                add(way, k, a)
+                if k < n - 1:
+                    ring(way, k, a).start()
+                elif joined:
+                    trade(way, a).start()
+    for a in range(many):
+        if joined:
+            for way in range(2):
+                trade(way, a).wait()
+
+            def act(rows):
+                total = own[a][me, rows, :].astype(jnp.float32) + fresh[a][rows, :].astype(
+                    jnp.float32
+                )
+                own[a][me, rows, :] = total.astype(jnp.bfloat16)
+
+            sweep(a, act)
+        put(a).start()
+        back(a, core).start()
+    for a in range(many):
+        put(a).wait()
+        back(a, core).wait_send()
+        back(a, 1 - core).wait_recv()
+    for k in range(n - 1):
+        for a in range(many):
+            for way in range(2):
+                ring(way, k, a).wait_send()
+    for j, b in enumerate(order):
+        for a in range(many):
+            across(j, b, a).wait_send()
+
+
+def reduce_all(grads):
+    n, many = lax.axis_size("seq"), len(grads)
+    joined = lax.axis_size("dp") == 4
+    blocks = [grad.reshape(n, -1, grad.shape[-1]) for grad in grads]
+    anywhere = pl.BlockSpec(memory_space=pl.ANY)
+
+    def buffers(count, way=None):
+        shapes = []
+        for part in blocks:
+            width = part.shape[2] if way is None else halves(part.shape[2])[way][1]
+            lead = () if count is None else (count,)
+            shapes.append(pltpu.VMEM((*lead, part.shape[1] // 2, width), jnp.bfloat16))
+        return shapes
+
+    dma = pltpu.SemaphoreType.DMA
+    sums = pl.pallas_call(
+        functools.partial(reduce_kernel, n, many, joined),
+        out_shape=[jax.ShapeDtypeStruct(part.shape[1:], jnp.bfloat16) for part in blocks],
+        in_specs=[anywhere] * many,
+        out_specs=[anywhere] * many,
+        scratch_shapes=[
+            *buffers(n),
+            *buffers(n),
+            *buffers(n - 1, 0),
+            *buffers(n - 1, 1),
+            *buffers(None),
+            dma((n, many)),
+            dma((n, many)),
+            dma((n, many)),
+            dma((2, n - 1, many)),
+            dma((2, n - 1, many)),
+            dma((2, many)),
+            dma((2, many)),
+            dma((many,)),
+            dma((many,)),
+            dma((many,)),
+        ],
+        compiler_params=pltpu.CompilerParams(
+            collective_id=3, has_side_effects=True, vmem_limit_bytes=48 * 2**20
+        ),
+    )(*blocks)
+    if joined:
+        return sums
+    core = lax.axis_index("dp") % 2
+    total = []
+    for part in sums:
+        rows = lax.broadcasted_iota(jnp.int32, part.shape, 0)
+        mine = rows // (part.shape[0] // 2) == core
+        total.append(lax.psum(jnp.where(mine, part, 0).astype(jnp.bfloat16), "dp"))
+    return total
+
+
+def scan_kernel(n, reverse, x_ref, y_ref, held, sent, send_sem, recv_sem, out_send, out_recv):
+    me, replica = lax.axis_index("seq"), lax.axis_index("dp")
+    share = x_ref.shape[0] // n
+    width = y_ref.shape[1]
+    greet([((me + off) % n, replica) for off in range(1, n)])
+
+    def span(index):
+        return pl.ds(index * share, share)
+
+    def spread(off):
+        target = (me + off) % n
+        return pltpu.make_async_remote_copy(
+            src_ref=x_ref.at[span(target)],
+            dst_ref=held.at[me],
+            send_sem=send_sem.at[off - 1],
+            recv_sem=recv_sem.at[off - 1],
+            device_id=(target, replica),
+            device_id_type=MESH,
+        )
+
+    def arrive(off):
+        source = (me + n - off) % n
+        return pltpu.make_async_remote_copy(
+            src_ref=x_ref.at[span(me)],
+            dst_ref=held.at[source],
+            send_sem=send_sem.at[off - 1],
+            recv_sem=recv_sem.at[off - 1],
+            device_id=(source, replica),
+            device_id_type=MESH,
+        )
+
+    def give(off):
+        target = (me + off) % n
+        return pltpu.make_async_remote_copy(
+            src_ref=sent.at[target],
+            dst_ref=y_ref.at[span(me)],
+            send_sem=out_send.at[off - 1],
+            recv_sem=out_recv.at[off - 1],
+            device_id=(target, replica),
+            device_id_type=MESH,
+        )
+
+    def take(off):
+        source = (me + n - off) % n
+        return pltpu.make_async_remote_copy(
+            src_ref=sent.at[me],
+            dst_ref=y_ref.at[span(source)],
+            send_sem=out_send.at[off - 1],
+            recv_sem=out_recv.at[off - 1],
+            device_id=(source, replica),
+            device_id_type=MESH,
+        )
+
+    for off in range(1, n):
+        spread(off).start()
+    held[me] = x_ref[span(me)]
+    for off in range(1, n):
+        arrive(off).wait_recv()
+    for p in range(share):
+        state = jnp.zeros(y_ref.shape[1:], jnp.float32)
+        for s in range(n - 1, -1, -1) if reverse else range(n):
+            sent[s, p] = state.astype(sent.dtype)
+            passing = held[s, p, width : width + ROWS].astype(jnp.float32)[:1]
+            state = passing * state + held[s, p, :width].astype(jnp.float32)
+    for off in range(1, n):
+        give(off).start()
+    y_ref[span(me)] = sent[me]
+    for off in range(1, n):
+        take(off).wait_recv()
+    for off in range(1, n):
+        spread(off).wait_send()
+        give(off).wait_send()
+
+
+def entering(passing, deposit, reverse):
+    n = lax.axis_size("seq")
+    seqs, heads, values, keys = deposit.shape
+    pairs = seqs * heads
+    share = pairs // n
+    tail = jnp.broadcast_to(passing.reshape(pairs, 1, keys), (pairs, ROWS, keys))
+    packed = jnp.concatenate([deposit.reshape(pairs, values, keys), tail], axis=1)
+    dma = pltpu.SemaphoreType.DMA((n - 1,))
+    arrived = pl.pallas_call(
+        functools.partial(scan_kernel, n, reverse),
+        out_shape=jax.ShapeDtypeStruct((pairs, values, keys), jnp.bfloat16),
+        in_specs=[pl.BlockSpec(memory_space=pltpu.VMEM)],
+        out_specs=pl.BlockSpec(memory_space=pltpu.VMEM),
+        scratch_shapes=[
+            pltpu.VMEM((n, share, values + ROWS, keys), jnp.bfloat16),
+            pltpu.VMEM((n, share, values, keys), jnp.bfloat16),
+            dma,
+            dma,
+            dma,
+            dma,
+        ],
+        compiler_params=pltpu.CompilerParams(
+            collective_id=2 if reverse else 1,
+            has_side_effects=True,
+            vmem_limit_bytes=16 * 2**20,
+        ),
+    )(packed.astype(jnp.bfloat16))
+    return arrived.reshape(seqs, heads, values, keys).swapaxes(2, 3).astype(jnp.float32)
 
 
 def matmul(left, right):
@@ -88,10 +482,6 @@
 def head_norm_back(grad_unit, unit, scale):
     live = jnp.where(scale < 1.0, 1.0, 0.0)
     return scale * (grad_unit - live * unit * jnp.mean(grad_unit * unit, axis=-1, keepdims=True))
-
-
-def compose(earlier, later):
-    return (earlier[0] * later[0], later[0][..., None] * earlier[1] + later[1])
 
 
 def block_step(memory, pieces):
@@ -169,13 +559,10 @@
     ending = running[:, -1]
     weighted_keys = jnp.exp(ending[:, None] - running) * key_float.reshape(seqs, span, HEADS, KH)
     deposit = jnp.einsum(
-        "snhk,snhv->shkv", weighted_keys, value_float.reshape(seqs, span, HEADS, VH), precision=HIGH
+        "snhk,snhv->shvk", weighted_keys, value_float.reshape(seqs, span, HEADS, VH), precision=HIGH
     )
     passing = jnp.exp(ending)
-    arrived = entering(
-        (passing, deposit), "seq", compose, (jnp.ones_like(passing), jnp.zeros_like(deposit))
-    )
-    memory_in = arrived[1]
+    memory_in = entering(passing, deposit, False)
     mixed, memory_out = span_attention(scaled_queries, key_float, value_float, log_decay, memory_in)
     mixed_heads = mixed.reshape(count, HEADS, VH)
     scale_heads = head_scale(mixed_heads)
@@ -290,21 +677,19 @@
     )
     growth = jnp.exp(running)
     local_pull = jnp.einsum(
-        "snhk,snhv->shkv",
+        "snhk,snhv->shvk",
         scaled_queries.reshape(seqs, span, HEADS, KH) * growth,
         grad_mixed.reshape(seqs, span, HEADS, VH),
         precision=HIGH,
     )
     passing = jnp.exp(running[:, -1])
-    returned = entering_2(
-        (passing, local_pull), "seq", compose, (jnp.ones_like(passing), jnp.zeros_like(local_pull))
-    )
+    returned = entering(passing, local_pull, True)
 
     def local_span(first, second, third, fourth):
         return span_attention(first, second, third, fourth, memory_in)
 
     unused, pullback = jax.vjp(local_span, scaled_queries, key_float, value_float, log_decay)
-    grad_scaled, grad_key_float, grad_value_float, grad_decay = pullback((grad_mixed, returned[1]))
+    grad_scaled, grad_key_float, grad_value_float, grad_decay = pullback((grad_mixed, returned))
     grad_queries = (grad_scaled.reshape(count, HEADS * KH) * KH ** (-0.5)).astype(jnp.bfloat16)
     grad_keys = grad_key_float.reshape(count, HEADS * KH).astype(jnp.bfloat16)
     grad_values = grad_value_float.reshape(count, HEADS * VH).astype(jnp.bfloat16)
@@ -371,101 +756,76 @@
     w_up,
     w_down,
 ):
+    n = lax.axis_size("seq")
+    gains = (attn_gain, w_rank_out, rank_bias, out_gain, mlp_gain)
+    rows = w_query.shape[0]
+    flat = jnp.concatenate([gain.reshape(-1) for gain in gains])
+    flat = jnp.pad(flat, (0, rows * SMALL - flat.size)).reshape(rows, SMALL)
+    spare = jnp.zeros((rows, 128 - w_rank_in.shape[1] - SMALL), w_query.dtype)
+    mixer = jnp.concatenate([w_query, w_key, w_value, w_gate, w_out, w_rank_in, flat, spare], axis=1)
+    up_pair = jnp.concatenate([w_gate_ff, w_up], axis=1)
+    mixer, up_pair, down = gather_all([mixer, up_pair, w_down])
+    cuts = [0]
+    for weight in (w_query, w_key, w_value, w_gate, w_out, w_rank_in):
+        cuts.append(cuts[-1] + weight.shape[1])
+    parts = [mixer[:, low:high] for low, high in zip(cuts[:-1], cuts[1:])]
+    flat = mixer[:, cuts[-1] : cuts[-1] + SMALL].reshape(n, rows * SMALL)
+    small, at = [], 0
+    for gain in gains:
+        piece = flat[:, at : at + gain.size].reshape(n * gain.shape[0], *gain.shape[1:])
+        small.append(piece)
+        at += gain.size
     whole = (
-        lax.all_gather(attn_gain, "seq", axis=0, tiled=True),
-        lax.all_gather(w_query, "seq", axis=0, tiled=True),
-        lax.all_gather(w_key, "seq", axis=0, tiled=True),
-        lax.all_gather(w_value, "seq", axis=0, tiled=True),
-        lax.all_gather(w_gate, "seq", axis=0, tiled=True),
-        lax.all_gather(w_rank_in, "seq", axis=0, tiled=True),
-        lax.all_gather(w_rank_out, "seq", axis=0, tiled=True),
-        lax.all_gather(rank_bias, "seq", axis=0, tiled=True),
-        lax.all_gather(out_gain, "seq", axis=0, tiled=True),
-        lax.all_gather(w_out, "seq", axis=0, tiled=True),
-        lax.all_gather(mlp_gain, "seq", axis=0, tiled=True),
-        lax.all_gather(w_gate_ff, "seq", axis=0, tiled=True),
-        lax.all_gather(w_up, "seq", axis=0, tiled=True),
-        lax.all_gather(w_down, "seq", axis=0, tiled=True),
+        small[0],
+        parts[0],
+        parts[1],
+        parts[2],
+        parts[3],
+        parts[5],
+        small[1],
+        small[2],
+        small[3],
+        parts[4],
+        small[4],
+        up_pair[:, : w_gate_ff.shape[1]],
+        up_pair[:, w_gate_ff.shape[1] :],
+        down,
     )
     kept = forward(whole, inputs)
     output = kept[-1]
-    whole = (
-        lax.all_gather(attn_gain, "seq", axis=0, tiled=True),
-        lax.all_gather(w_query, "seq", axis=0, tiled=True),
-        lax.all_gather(w_key, "seq", axis=0, tiled=True),
-        lax.all_gather(w_value, "seq", axis=0, tiled=True),
-        lax.all_gather(w_gate, "seq", axis=0, tiled=True),
-        lax.all_gather(w_rank_in, "seq", axis=0, tiled=True),
-        lax.all_gather(w_rank_out, "seq", axis=0, tiled=True),
-        lax.all_gather(rank_bias, "seq", axis=0, tiled=True),
-        lax.all_gather(out_gain, "seq", axis=0, tiled=True),
-        lax.all_gather(w_out, "seq", axis=0, tiled=True),
-        lax.all_gather(mlp_gain, "seq", axis=0, tiled=True),
-        lax.all_gather(w_gate_ff, "seq", axis=0, tiled=True),
-        lax.all_gather(w_up, "seq", axis=0, tiled=True),
-        lax.all_gather(w_down, "seq", axis=0, tiled=True),
-    )
-    kept = forward(whole, inputs)
     grads, input_grad = backward(whole, kept, cotangent)
-    owned = (
-        lax.psum_scatter(
-            grads[0].astype(jnp.bfloat16), "seq", scatter_dimension=0, tiled=True
-        ).astype(jnp.float32),
-        lax.psum_scatter(
-            grads[1].astype(jnp.bfloat16), "seq", scatter_dimension=0, tiled=True
-        ).astype(jnp.float32),
-        lax.psum_scatter(
-            grads[2].astype(jnp.bfloat16), "seq", scatter_dimension=0, tiled=True
-        ).astype(jnp.float32),
-        lax.psum_scatter(
-            grads[3].astype(jnp.bfloat16), "seq", scatter_dimension=0, tiled=True
-        ).astype(jnp.float32),
-        lax.psum_scatter(
-            grads[4].astype(jnp.bfloat16), "seq", scatter_dimension=0, tiled=True
-        ).astype(jnp.float32),
-        lax.psum_scatter(
-            grads[5].astype(jnp.bfloat16), "seq", scatter_dimension=0, tiled=True
-        ).astype(jnp.float32),
-        lax.psum_scatter(
-            grads[6].astype(jnp.bfloat16), "seq", scatter_dimension=0, tiled=True
-        ).astype(jnp.float32),
-        lax.psum_scatter(
-            grads[7].astype(jnp.bfloat16), "seq", scatter_dimension=0, tiled=True
-        ).astype(jnp.float32),
-        lax.psum_scatter(
-            grads[8].astype(jnp.bfloat16), "seq", scatter_dimension=0, tiled=True
-        ).astype(jnp.float32),
-        lax.psum_scatter(
-            grads[9].astype(jnp.bfloat16), "seq", scatter_dimension=0, tiled=True
-        ).astype(jnp.float32),
-        lax.psum_scatter(
-            grads[10].astype(jnp.bfloat16), "seq", scatter_dimension=0, tiled=True
-        ).astype(jnp.float32),
-        lax.psum_scatter(
-            grads[11].astype(jnp.bfloat16), "seq", scatter_dimension=0, tiled=True
-        ).astype(jnp.float32),
-        lax.psum_scatter(
-            grads[12].astype(jnp.bfloat16), "seq", scatter_dimension=0, tiled=True
-        ).astype(jnp.float32),
-        lax.psum_scatter(
-            grads[13].astype(jnp.bfloat16), "seq", scatter_dimension=0, tiled=True
-        ).astype(jnp.float32),
-    )
+    low = [grad.astype(jnp.bfloat16) for grad in grads]
+    flat = jnp.concatenate(
+        [low[i].reshape(n, -1) for i in (0, 6, 7, 8, 10)], axis=1
+    )
+    flat = jnp.pad(flat, ((0, 0), (0, rows * SMALL - flat.shape[1]))).reshape(n * rows, SMALL)
+    spare = jnp.zeros((n * rows, spare.shape[1]), jnp.bfloat16)
+    mixer = jnp.concatenate(
+        [low[1], low[2], low[3], low[4], low[9], low[5], flat, spare], axis=1
+    )
+    mixer, up_pair, down = reduce_all([mixer, jnp.concatenate([low[11], low[12]], axis=1), low[13]])
+    mixer, up_pair = mixer.astype(jnp.float32), up_pair.astype(jnp.float32)
+    parts = [mixer[:, start:end] for start, end in zip(cuts[:-1], cuts[1:])]
+    flat = mixer[:, cuts[-1] : cuts[-1] + SMALL].reshape(-1)
+    small, at = [], 0
+    for gain in gains:
+        small.append(flat[at : at + gain.size].reshape(gain.shape))
+        at += gain.size
     summed = (
-        lax.psum(owned[0].astype(jnp.bfloat16), "dp").astype(jnp.float32),
-        lax.psum(owned[1].astype(jnp.bfloat16), "dp").astype(jnp.float32),
-        lax.psum(owned[2].astype(jnp.bfloat16), "dp").astype(jnp.float32),
-        lax.psum(owned[3].astype(jnp.bfloat16), "dp").astype(jnp.float32),
-        lax.psum(owned[4].astype(jnp.bfloat16), "dp").astype(jnp.float32),
-        lax.psum(owned[5].astype(jnp.bfloat16), "dp").astype(jnp.float32),
-        lax.psum(owned[6].astype(jnp.bfloat16), "dp").astype(jnp.float32),
-        lax.psum(owned[7].astype(jnp.bfloat16), "dp").astype(jnp.float32),
-        lax.psum(owned[8].astype(jnp.bfloat16), "dp").astype(jnp.float32),
-        lax.psum(owned[9].astype(jnp.bfloat16), "dp").astype(jnp.float32),
-        lax.psum(owned[10].astype(jnp.bfloat16), "dp").astype(jnp.float32),
-        lax.psum(owned[11].astype(jnp.bfloat16), "dp").astype(jnp.float32),
-        lax.psum(owned[12].astype(jnp.bfloat16), "dp").astype(jnp.float32),
-        lax.psum(owned[13].astype(jnp.bfloat16), "dp").astype(jnp.float32),
+        small[0],
+        parts[0],
+        parts[1],
+        parts[2],
+        parts[3],
+        parts[5],
+        small[1],
+        small[2],
+        small[3],
+        parts[4],
+        small[4],
+        up_pair[:, : w_gate_ff.shape[1]],
+        up_pair[:, w_gate_ff.shape[1] :],
+        down.astype(jnp.float32),
     )
     return (
         output,

time: 1550 us -> 664 us (0.43)
  waiting for transfers between devices: 1090 us -> 0 us
  Pallas kernels: 0 us -> 425 us
  blocking collectives: 179 us -> 0 us
  other arithmetic: 59.9 us -> 32.1 us
  local copies, waits for them, and re-layouts: 64.4 us -> 86.4 us
  between operations: 19.4 us -> 1.87 us
  matrix products: 123 us -> 107 us
    reduce_scatter x8 -> x0, waiting for transfers between devices: 592 us -> none  [the longest x1 113 us: body(): lax.psum_scatter(grads[12].astype(jnp.bfloat16), 'seq', scatter_dimension...]
    pallas_call x0 -> x4, Pallas kernels: none -> 425 us  [the longest x1 213 us: gather_all(): pl.pallas_call(functools.partial(gather_kernel, n, many), out_shape=[jax....]
    all_gather x10 -> x0, waiting for transfers between devices: 407 us -> none  [the longest x1 88.8 us: body(): lax.all_gather(w_gate_ff, 'seq', axis=0, tiled=True)]
    all_gather x5 -> x0, blocking collectives: 114 us -> none  [the longest x1 26.5 us: entering(): lax.all_gather(part.astype(kind), axis)]
    psum x1 -> x0, waiting for transfers between devices: 62.8 us -> none  [body(): lax.psum(owned[1].astype(jnp.bfloat16), 'dp').astype(jnp.float32)]
    unnamed x2 -> x0, blocking collectives: 59.2 us -> none
    unnamed x21 -> x0, waiting for transfers between devices: 28.3 us -> none
    concatenate x0 -> x5, local copies, waits for them, and re-layouts: none -> 19.8 us  [the longest x2 13.8 us: body(): jnp.concatenate([low[1], low[2], low[3], low[4], low[9], low[5], flat, sp...]
  transfers between devices with their start and end apart: 20 -> 0, of which waited for: 17 -> 0; matrix products, arithmetic and copies ran while one was open for 13% -> 0% of each run, Pallas kernels for 0% -> 0%
where the time goes in v1:
time: 664 us; the launch traced here: 653 us
  Pallas kernels  425 us (64%)
  matrix products  107 us (16%)
  local copies, waits for them, and re-layouts  86.4 us (13%)
  other arithmetic  32.1 us (5%)
    pallas_call x1, Pallas kernels, gather_all(): pl.pallas_call(functools.partial(gather_kernel, n, many), out_shape=[jax....  213 us
    pallas_call x1, Pallas kernels, reduce_all(): pl.pallas_call(functools.partial(reduce_kernel, n, many, joined), out_sha...  159 us
    pallas_call x2, Pallas kernels, entering(): pl.pallas_call(functools.partial(scan_kernel, n, reverse), out_shape=jax....  53.5 us
    dot_general x9, matrix products, matmul(): return jnp.dot(left, right, preferred_element_type=jnp.float32)  26.5 us
    dot_general x8, matrix products, times_transposed(): lax.dot_general(left, right, (((1,), (1,)), ((), ())), preferred_element_...  19.3 us
    dot_general x8, matrix products, inner_rows(): lax.dot_general(left, right, (((0,), (0,)), ((), ())), preferred_element_...  16.9 us
    dot_general x8, matrix products, block_step(): deposit = jnp.einsum('bhsk,bhsv->bhkv', carried, values, precision=HIGH)  14.5 us
    squeeze x14, local copies, waits for them, and re-layouts, span_attention(): lax.scan(jax.checkpoint(block_step), memory_in, pieces)  14.1 us

profile of v1, /device:TPU:0, one launch (start us, length us, event | category | flops | bytes accessed | tf_op | source)
XLA Modules:
  0.0 652.8 jit_solution(78239368768218984)
XLA Ops:
  2.1 2.8 concatenate.41
  5.0 3.2 concatenate.42.refs_0_
  8.2 2.6 pad_maximum_fusion.1.refs_1_
  10.7 212.7 %shard_map.279 = (bf16[8,128,4224]{2,1,0:T(8,128)(2,1)}, bf16[8,128,5632]{2,1,0:T(8,128)(2,1)}, bf16[8,352,1024]{2,1,0:T(8,128)(2,1)}) custom-call(bf16[128,4224]{1,0:T(8,128)(2,1)} %concatenate.42.refs_0_, bf16[128,5632]{1,0:T(8,128)(2,1)} %pad_maximum_fusion.1.refs_1_, bf16[352,1024]{1,0:T(8,128)(2,1)} %refs_2_.1), custom_call_target="tpu_custom_call" | custom-call | tf_op jit(solution)/shard_map/pallas_call | solution.py:118
  239.7 23.6 %shard_map.280 = bf16[8,256,128]{2,1,0:T(8,128)(2,1)S(1)} custom-call(bf16[8,272,128]{2,1,0:T(8,128)(2,1)S(1)} %pad_maximum_fusion.3.x_ref), custom_call_target="tpu_custom_call" | custom-call | tf_op jit(solution)/shard_map/pallas_call | solution.py:432
  273.9 2.5 reshape.406
  278.8 18.8 %while.49 = (s32[]{:T(128)}, f32[2,4,128,256]{3,2,1,0:T(8,128)S(1)}, f32[2,2,4,64,256]{4,3,2,1,0:T(8,128)}, f32[2,2,4,64,128]{4,3,2,1,0:T(8,128)}, f32[2,2,4,64,...) while((s32[]{:T(128)}, ...), condition=%wide.region_4.5_spmd.clone, body=%wide.region_2.4_spmd.sunk.clone | while | flops 558866432 | bytes 13446269 | solution.py:519
  283.4 2.5 fusion.239
  292.7 2.5 fusion.239
  302.6 2.7 multiply_convert_fusion.6
  307.7 6.0 convolution_bitcast_fusion
  314.7 3.2 fusion.38
  317.9 5.2 multiply_convert_fusion.1
  323.2 6.8 %fusion.64 = bf16[256,1024]{1,0:T(8,128)(2,1)} fusion(f32[256,1024]{1,0:T(8,128)S(1)} %get-tuple-element.517, bf16[256,2816]{1,0:T(8,128)(2,1)S(1)} %get-tuple-element.489, bf16[2816,1024]{1,0:T(8,128)(2,1)} %bitcast.467), kind=kOutput, calls=%fused_computation.111 | convolution fusion | flops 1476919296 | bytes 8781824 | tf_op jit(solution)/shard_map/dot_general | solution.py:455
  338.8 2.8 reshape.390
  347.4 29.8 %shard_map.281 = bf16[8,256,128]{2,1,0:T(8,128)(2,1)S(1)} custom-call(bf16[8,272,128]{2,1,0:T(8,128)(2,1)S(1)} %pad_maximum_fusion.2.x_ref), custom_call_target="tpu_custom_call" | custom-call | tf_op jit(solution)/shard_map/pallas_call | solution.py:432
  379.1 9.6 %while.50 = (s32[]{:T(128)}, f32[2,4,128,256]{3,2,1,0:T(8,128)S(1)}, f32[2,2,4,128,256]{4,3,2,1,0:T(8,128)}, f32[2,2,4,64,128]{4,3,2,1,0:T(8,128)}, f32[2,2,4,64...) while((s32[]{:T(128)}, f32[2,4,128,256]{3,2,1,0:T(8,128)S(1)}, ...), condition=%wide.region_11.12_spmd.clone, body=%wide.region_9.11_spmd.sunk.clone | while | flops 206110720 | bytes 6317145 | solution.py:519
  390.5 2.7 fusion.81
  394.9 38.1 %while.51 = (s32[]{:T(128)}, f32[2,4,128,256]{3,2,1,0:T(8,128)S(1)}, f32[2,2,4,64,128]{4,3,2,1,0:T(8,128)}, bf16[2,2,4,64,128]{4,3,2,1,0:T(8,128)(2,1)}, bf16[2,...) while((s32[]{:T(128)}, ...), condition=%wide.region_17.18_spmd.clone, body=%wide.region_12.17_spmd.sunk.clone | while | flops 1169301504 | bytes 49136044 | solution.py:519
  454.8 13.6 %concatenate.54.refs_0_ = bf16[8,128,4224]{2,1,0:T(8,128)(2,1)} concatenate(bf16[8,128,512]{2,1,0:T(8,128)(2,1)} %bitcast.408, bf16[8,128,512]{2,1,0:T(8,128)(2,1)} %bitcast.409, bf16[8,128,1024]{2,1,0:T(8,128)(2,1)} %bitcast.403, bf16[8,128,1024]{2,1,0:T(8,128)(2,1)} %bitcast.404, bf16[8,128,1024]{2,1,0:T(8,128)(2,1)S(1)} %bitcast.402, bf16[8,128,16]{2,1,0:T(8,128)(2,1)S(1)} %bitcast.431, ...), dimensions={2} | concatenate | bytes 17301504 | tf_op jit(solution)/shard_map/concatenate | solution.py:803
  468.4 3.2 convolution_convert_fusion.1
  473.3 7.2 %pad_maximum_fusion = bf16[1024,5632]{1,0:T(8,128)(2,1)} fusion(bf16[1024,2816]{1,0:T(8,128)(2,1)S(1)} %convolution_convert_fusion.1, bf16[1024,2816]{1,0:T(8,128)(2,1)S(1)} %convolution_convert_fusion.2), kind=kLoop, calls=%fused_computation.68 | loop fusion | flops 23068672 | bytes 23068672 | tf_op jit(solution)/shard_map/concatenate | solution.py:806
  480.5 4.2 convolution_convert_fusion
  484.7 158.6 %shard_map.282 = (bf16[128,4224]{1,0:T(8,128)(2,1)S(1)}, bf16[128,5632]{1,0:T(8,128)(2,1)S(1)}, bf16[352,1024]{1,0:T(8,128)(2,1)S(1)}) custom-call(bf16[8,128,4224]{2,1,0:T(8,128)(2,1)} %concatenate.54.refs_0_, bf16[8,128,5632]{2,1,0:T(8,128)(2,1)} %bitcast.396, bf16[8,352,1024]{2,1,0:T(8,128)(2,1)} %bitcast.397), custom_call_target="tpu_custom_call" | custom-call | tf_op jit(solution)/shard_map/pallas_call | solution.py:313
  (306 shorter events, 151.6 us)
Async XLA Ops:
  8.2 217.0 %copy-start.4 = (bf16[2,128,1024]{2,1,0:T(8,128)(2,1)S(1)}, bf16[2,128,1024]{2,1,0:T(8,128)(2,1)}, u32[]{:S(2)}) copy-start(bf16[2,128,1024]{2,1,0:T(8,128)(2,1)} %param.22) | copy-start | bytes 1572868
  225.6 10.7 %copy-start.9 = (bf16[256,1024]{1,0:T(8,128)(2,1)}, bf16[256,1024]{1,0:T(8,128)(2,1)S(1)}, u32[]{:S(2)}) copy-start(bf16[256,1024]{1,0:T(8,128)(2,1)S(1)} %multiply_convert_fusion.7) | copy-start | bytes 1572868
  238.6 24.9 %copy-start.16 = (bf16[256,1024]{1,0:T(8,128)(2,1)}, bf16[256,1024]{1,0:T(8,128)(2,1)S(1)}, u32[]{:S(2)}) copy-start(bf16[256,1024]{1,0:T(8,128)(2,1)S(1)} %fusion.65) | copy-start | bytes 1572868
  280.0 5.9 copy-start
  289.4 5.9 copy-start
  302.6 4.3 copy-start.36
  305.3 8.4 %copy-start.37 = (bf16[256,1024]{1,0:T(8,128)(2,1)}, bf16[256,1024]{1,0:T(8,128)(2,1)S(1)}, u32[]{:S(2)}) copy-start(bf16[256,1024]{1,0:T(8,128)(2,1)S(1)} %get-tuple-element.479) | copy-start | bytes 1572868
  307.7 7.0 %copy-start.42 = (bf16[8,128,5632]{2,1,0:T(8,128)(2,1)S(1)}, bf16[8,128,5632]{2,1,0:T(8,128)(2,1)}, u32[]{:S(2)}) copy-start(bf16[8,128,5632]{2,1,0:T(8,128)(2,1)} %get-tuple-element.339) | copy-start | bytes 34603012
  313.9 4.0 copy-start.12
  323.1 6.8 %copy-start.14 = (bf16[256,2816]{1,0:T(8,128)(2,1)}, bf16[256,2816]{1,0:T(8,128)(2,1)S(1)}, u32[]{:S(2)}) copy-start(bf16[256,2816]{1,0:T(8,128)(2,1)S(1)} %get-tuple-element.489) | copy-start | bytes 4325380
  323.2 6.8 %copy-start.30 = (bf16[256,2816]{1,0:T(8,128)(2,1)}, bf16[256,2816]{1,0:T(8,128)(2,1)S(1)}, u32[]{:S(2)}) copy-start(bf16[256,2816]{1,0:T(8,128)(2,1)S(1)} %get-tuple-element.490) | copy-start | bytes 4325380
  323.2 8.5 %copy-start.28 = (bf16[256,2816]{1,0:T(8,128)(2,1)}, bf16[256,2816]{1,0:T(8,128)(2,1)S(1)}, u32[]{:S(2)}) copy-start(bf16[256,2816]{1,0:T(8,128)(2,1)S(1)} %get-tuple-element.488) | copy-start | bytes 4325380
  394.9 4.2 copy-start.1
  394.9 5.1 copy-start.6
  408.6 4.4 copy-start.23
  413.9 4.2 copy-start.1
  413.9 5.1 copy-start.6
  427.5 4.4 copy-start.23
  433.0 4.0 copy-start.19
  434.6 4.4 copy-start.34
  448.4 4.2 copy-start.38
  454.8 13.6 %copy-start.13 = (bf16[256,1024]{1,0:T(8,128)(2,1)S(1)}, bf16[256,1024]{1,0:T(8,128)(2,1)}, u32[]{:S(2)}) copy-start(bf16[256,1024]{1,0:T(8,128)(2,1)} %copy-done.12) | copy-start | bytes 1572868
  473.3 7.2 %copy-start.15 = (bf16[256,2816]{1,0:T(8,128)(2,1)S(1)}, bf16[256,2816]{1,0:T(8,128)(2,1)}, u32[]{:S(2)}) copy-start(bf16[256,2816]{1,0:T(8,128)(2,1)} %copy-done.14) | copy-start | bytes 4325380
  473.3 7.2 %copy-start.27 = (bf16[2,128,1024]{2,1,0:T(8,128)(2,1)S(1)}, bf16[2,128,1024]{2,1,0:T(8,128)(2,1)}, u32[]{:S(2)}) copy-start(bf16[2,128,1024]{2,1,0:T(8,128)(2,1)} %param.23) | copy-start | bytes 1572868
  (29 other events, 62.7 us)

commit v2 on v1

v2 whole, which is shorter than its diff:
```python
import functools

import jax
import jax.numpy as jnp
from jax import lax
from jax.experimental import pallas as pl
from jax.experimental.pallas import tpu as pltpu
from jax.sharding import PartitionSpec as P

HEADS = 4
KH = 128
VH = 256
BLOCK = 64


EPS = 1e-06
HIGH = lax.Precision.HIGHEST


MESH = pl.DeviceIdType.MESH
ROWS = 16
SMALL = 16
IN_VMEM = pl.BlockSpec(memory_space=pltpu.VMEM)


def ring_place(index, n):
    odd = index % 2
    return (1 - odd) * (index // 2) + odd * (n - 1 - index // 2)


def ring_index(place, n):
    place = (place + 2 * n) % n
    late = place // (n // 2)
    return (1 - late) * 2 * place + late * (2 * (n - 1 - place) + 1)


def greet(devices):
    barrier = pltpu.get_barrier_semaphore()
    for device in devices:
        pl.semaphore_signal(barrier, inc=1, device_id=device, device_id_type=MESH)
    pl.semaphore_wait(barrier, len(devices))


def split_columns(width):
    side = (width // 128 + 1) // 3 * 128
    return (side, width - 2 * side)


def partners(n):
    me, replica = lax.axis_index("seq"), lax.axis_index("dp")
    core, plane = replica % 2, (replica // 2) % 2
    place = ring_place(me, n)
    pair = (me, replica + 1 - 2 * core)
    peer = (me, replica + 2 - 4 * plane)
    onward = [(ring_index(place + 1, n), replica), (ring_index(place - 1, n), replica)]
    return (me, core, plane, place, pair, peer, onward)


def class_columns(width, way, plane):
    side, rest = split_columns(width)
    if way == 0:
        return pl.ds(pl.multiple_of(plane * side, 128), side)
    return pl.ds(2 * side, rest)


def cut(refs, sizes):
    pieces, at = [], 0
    for size in sizes:
        pieces.append(refs[at : at + size])
        at += size
    return (*pieces, refs[at:])


def everyone(n):
    me, replica = lax.axis_index("seq"), lax.axis_index("dp")
    return [((me + off) % n, replica) for off in range(1, n)]


def gather_kernel(n, many, layout, beside, given, made, *refs):
    shards, beside_in, wholes, beside_out, held, sems, beside_scratch = cut(
        refs, (len(layout), given, many, made, many, 9)
    )
    count = len(layout)
    work = beside(n, *beside_in, *beside_out, *beside_scratch) if beside else None
    (
        load_sem,
        own_sem,
        ring_send,
        ring_recv,
        peer_send,
        peer_recv,
        pair_send,
        pair_recv,
        out_sem,
    ) = sems
    me, core, plane, place, pair, peer, onward = partners(n)

    def load(i):
        a, start, width = layout[i]
        return pltpu.make_async_copy(
            shards[i], held[a].at[me, :, pl.ds(start, width)], load_sem.at[i]
        )

    for i in range(count):
        load(i).start()
    greet([*(everyone(n) if beside else onward), pair, peer])

    def half_rows(a, half):
        rows = held[a].shape[1] // 2
        return pl.ds(pl.multiple_of(half * rows, ROWS), rows)

    def block(way, k):
        return ring_index(place - k if way == 0 else place + k, n)

    def own(a):
        return pltpu.make_async_copy(held[a].at[me], wholes[a].at[me], own_sem.at[a])

    def remote(here, send, recv, device):
        return pltpu.make_async_remote_copy(
            src_ref=here,
            dst_ref=here,
            send_sem=send,
            recv_sem=recv,
            device_id=device,
            device_id_type=MESH,
        )

    def ring(way, k, a, arriving):
        columns = class_columns(held[a].shape[2], way, plane)
        here = held[a].at[block(way, k + 1 if arriving else k), half_rows(a, core), columns]
        return remote(here, ring_send.at[way, k, a], ring_recv.at[way, k, a], onward[way])

    def swap(k, a, side):
        columns = class_columns(held[a].shape[2], 0, side)
        here = held[a].at[block(0, k + 1), half_rows(a, core), columns]
        return remote(here, peer_send.at[k, a], peer_recv.at[k, a], peer)

    def group(a, way):
        side, rest = split_columns(held[a].shape[2])
        return pl.ds(0, 2 * side) if way == 0 else pl.ds(2 * side, rest)

    def across(way, k, a, half):
        here = held[a].at[block(way, k + 1), half_rows(a, half), group(a, way)]
        return remote(here, pair_send.at[way, k, a], pair_recv.at[way, k, a], pair)

    def put(way, k, a):
        where = (block(way, k + 1), slice(None), group(a, way))
        return pltpu.make_async_copy(
            held[a].at[where], wholes[a].at[where], out_sem.at[way, k, a]
        )

    for i in range(count):
        load(i).wait()
    for k in range(n + 2):
        for a in range(many):
            for way in range(2):
                if 0 <= k - 1 < n - 1:
                    ring(way, k - 1, a, True).wait_recv()
                if k < n - 1:
                    ring(way, k, a, False).start()
                if 0 <= k - 1 < n - 1:
                    if way == 0:
                        swap(k - 1, a, plane).start()
                    else:
                        across(1, k - 1, a, core).start()
        if k == 0:
            for a in range(many):
                own(a).start()
        for a in range(many):
            if 0 <= k - 2 < n - 1:
                swap(k - 2, a, 1 - plane).wait_recv()
                across(0, k - 2, a, core).start()
        for a in range(many):
            for way in range(2):
                if 0 <= k - 3 < n - 1:
                    across(way, k - 3, a, 1 - core).wait_recv()
                    put(way, k - 3, a).start()
        if work:
            work(k)
    for k in range(n - 1):
        for a in range(many):
            swap(k, a, plane).wait_send()
            for way in range(2):
                ring(way, k, a, False).wait_send()
                across(way, k, a, core).wait_send()
                put(way, k, a).wait()
    for a in range(many):
        own(a).wait()


def gather_all(groups, collective_id, beside=None, operands=(), results=(), scratch=()):
    n, many = lax.axis_size("seq"), len(groups)
    anywhere = pl.BlockSpec(memory_space=pl.ANY)
    dma = pltpu.SemaphoreType.DMA
    layout, shards, shapes = [], [], []
    for a, group in enumerate(groups):
        start = 0
        for shard in group:
            layout.append((a, start, shard.shape[1]))
            shards.append(shard)
            start += shard.shape[1]
        shapes.append((n, group[0].shape[0], start))
    ring, single = dma((2, n - 1, many)), dma((n - 1, many))
    wholes = pl.pallas_call(
        functools.partial(
            gather_kernel, n, many, tuple(layout), beside, len(operands), len(results)
        ),
        out_shape=[*[jax.ShapeDtypeStruct(shape, jnp.bfloat16) for shape in shapes], *results],
        in_specs=[anywhere] * len(shards) + [IN_VMEM] * len(operands),
        out_specs=[anywhere] * many + [IN_VMEM] * len(results),
        scratch_shapes=[
            *[pltpu.VMEM(shape, jnp.bfloat16) for shape in shapes],
            dma((len(shards),)),
            dma((many,)),
            ring,
            ring,
            single,
            single,
            ring,
            ring,
            ring,
            *scratch,
        ],
        compiler_params=pltpu.CompilerParams(
            collective_id=collective_id, has_side_effects=True, vmem_limit_bytes=48 * 2**20
        ),
    )(*shards, *operands)
    return [*[whole.reshape(-1, whole.shape[-1]) for whole in wholes[:many]], *wholes[many:]]


def reduce_kernel(n, many, joined, beside, given, made, *refs):
    grads, beside_in, sums, beside_out, buffers, sems, beside_scratch = cut(
        refs, (many, given, many, made, 7 * many, 12)
    )
    work = beside(n, *beside_in, *beside_out, *beside_scratch) if beside else None
    own, other, first, second, swapped, fresh, landed, _ = cut(buffers, (many,) * 7)
    (
        local_sem,
        pair_send,
        pair_recv,
        ring_send,
        ring_recv,
        swap_send,
        swap_recv,
        peer_send,
        peer_recv,
        back_send,
        back_recv,
        out_sem,
    ) = sems
    moving = (first, second)
    me, core, plane, place, pair, peer, onward = partners(n)
    greet([*(everyone(n) if beside else onward), pair, peer])

    def rows_of(a, half):
        rows = grads[a].shape[1] // 2
        return pl.ds(pl.multiple_of(half * rows, ROWS), rows)

    def columns(a, way, side=None):
        return class_columns(grads[a].shape[2], way, plane if side is None else side)

    def block(way, k):
        return ring_index(place - 1 - k if way == 0 else place + 1 + k, n)

    def remote(source, target, send, recv, device):
        return pltpu.make_async_remote_copy(
            src_ref=source,
            dst_ref=target,
            send_sem=send,
            recv_sem=recv,
            device_id=device,
            device_id_type=MESH,
        )

    def load(j, b, a):
        return pltpu.make_async_copy(
            grads[a].at[b, rows_of(a, core)], own[a].at[b], local_sem.at[j, a]
        )

    def across(j, b, a):
        return remote(
            grads[a].at[b, rows_of(a, 1 - core)],
            other[a].at[b],
            pair_send.at[j, a],
            pair_recv.at[j, a],
            pair,
        )

    def ring(way, k, a):
        source = own[a].at[block(way, 0), :, columns(a, way)] if k == 0 else moving[way][a].at[k - 1]
        return remote(
            source,
            moving[way][a].at[k],
            ring_send.at[way, k, a],
            ring_recv.at[way, k, a],
            onward[way],
        )

    def swap(k, a):
        return remote(
            own[a].at[block(0, k), :, columns(a, 0, 1 - plane)],
            swapped[a].at[k],
            swap_send.at[k, a],
            swap_recv.at[k, a],
            peer,
        )

    def trade(a):
        return remote(
            own[a].at[me, :, columns(a, 1)],
            fresh[a],
            peer_send.at[1, a],
            peer_recv.at[1, a],
            peer,
        )

    def finish(a):
        here = own[a].at[me, :, columns(a, 0)]
        return remote(here, landed[a], peer_send.at[0, a], peer_recv.at[0, a], peer)

    def put(a):
        return pltpu.make_async_copy(own[a].at[me], sums[a].at[rows_of(a, core)], out_sem.at[a])

    def back(a, half):
        return remote(
            own[a].at[me], sums[a].at[rows_of(a, half)], back_send.at[a], back_recv.at[a], pair
        )

    def sweep(a, act):
        def turn(i, carry):
            act(pl.ds(pl.multiple_of(i * ROWS, ROWS), ROWS))
            return carry

        lax.fori_loop(0, grads[a].shape[1] // 2 // ROWS, turn, 0)

    order = []
    for k in range(n // 2):
        order.append(block(0, k))
        if len(order) < n - 1:
            order.append(block(1, k))
    order = order[: n - 1] + [me]
    for j, b in enumerate(order):
        for a in range(many):
            across(j, b, a).start()
            load(j, b, a).start()

    ready = set()

    def need(j, a):
        if (j, a) not in ready:
            ready.add((j, a))
            load(j, order[j], a).wait()
            across(j, order[j], a).wait_recv()

    def slot(way, k):
        if k == n - 1:
            return n - 1
        return 2 * k + way if 2 * k + way < n - 1 and k < n // 2 else 2 * (n - 2 - k) + 1 - way

    def hand_over(k, a):
        need(slot(0, k), a)
        b, theirs = block(0, k), columns(a, 0, 1 - plane)

        def act(rows):
            total = own[a][b, rows, theirs].astype(jnp.float32)
            total = total + other[a][b, rows, theirs].astype(jnp.float32)
            own[a][b, rows, theirs] = total.astype(jnp.bfloat16)

        sweep(a, act)
        swap(k, a).start()

    def add(way, k, a):
        need(slot(way, k), a)
        b, mine = block(way, k), columns(a, way)
        if way == 0:
            swap(k, a).wait_recv()
        if k > 0:
            ring(way, k - 1, a).wait_recv()

        def act(rows):
            total = own[a][b, rows, mine].astype(jnp.float32)
            total = total + other[a][b, rows, mine].astype(jnp.float32)
            if way == 0:
                total = total + swapped[a][k, rows, :].astype(jnp.float32)
            if k > 0:
                total = total + moving[way][a][k - 1, rows, :].astype(jnp.float32)
            if k == 0 or k == n - 1:
                own[a][b, rows, mine] = total.astype(jnp.bfloat16)
            else:
                moving[way][a][k - 1, rows, :] = total.astype(jnp.bfloat16)

        sweep(a, act)

    for k in range(n):
        for a in range(many):
            if k == 0:
                hand_over(0, a)
        for a in range(many):
            for way in (1, 0):
                add(way, k, a)
                if k < n - 1:
                    ring(way, k, a).start()
            if k < n - 1:
                hand_over(k + 1, a)
            elif joined:
                swap(k, a).wait_send()
                finish(a).start()
                trade(a).start()
        if work:
            work(k)
    for a in range(many):
        if joined:
            trade(a).wait()
            finish(a).wait()
            shared, theirs = columns(a, 1), columns(a, 0, 1 - plane)

            def act(rows):
                total = own[a][me, rows, shared].astype(jnp.float32)
                total = total + fresh[a][rows, :].astype(jnp.float32)
                own[a][me, rows, shared] = total.astype(jnp.bfloat16)
                own[a][me, rows, theirs] = landed[a][rows, :]

            sweep(a, act)
        else:
            swap(n - 1, a).wait_send()
        put(a).start()
        back(a, core).start()
    for a in range(many):
        put(a).wait()
        back(a, core).wait_send()
        back(a, 1 - core).wait_recv()
    for k in range(n - 1):
        for a in range(many):
            swap(k, a).wait_send()
            for way in range(2):
                ring(way, k, a).wait_send()
    for j, b in enumerate(order):
        for a in range(many):
            across(j, b, a).wait_send()


def reduce_all(grads, collective_id, beside=None, operands=(), results=(), scratch=()):
    n, many = lax.axis_size("seq"), len(grads)
    joined = lax.axis_size("dp") == 4
    blocks = [grad.reshape(n, -1, grad.shape[-1]) for grad in grads]
    anywhere = pl.BlockSpec(memory_space=pl.ANY)

    def buffers(count, way=None):
        shapes = []
        for part in blocks:
            width = part.shape[2] if way is None else split_columns(part.shape[2])[way]
            lead = () if count is None else (count,)
            shapes.append(pltpu.VMEM((*lead, part.shape[1] // 2, width), jnp.bfloat16))
        return shapes

    dma = pltpu.SemaphoreType.DMA
    sums = pl.pallas_call(
        functools.partial(reduce_kernel, n, many, joined, beside, len(operands), len(results)),
        out_shape=[
            *[jax.ShapeDtypeStruct(part.shape[1:], jnp.bfloat16) for part in blocks],
            *results,
        ],
        in_specs=[anywhere] * many + [IN_VMEM] * len(operands),
        out_specs=[anywhere] * many + [IN_VMEM] * len(results),
        scratch_shapes=[
            *buffers(n),
            *buffers(n),
            *buffers(n - 1, 0),
            *buffers(n - 1, 1),
            *buffers(n, 0),
            *buffers(None, 1),
            *buffers(None, 0),
            dma((n, many)),
            dma((n, many)),
            dma((n, many)),
            dma((2, n - 1, many)),
            dma((2, n - 1, many)),
            dma((n, many)),
            dma((n, many)),
            dma((2, many)),
            dma((2, many)),
            dma((many,)),
            dma((many,)),
            dma((many,)),
            *scratch,
        ],
        compiler_params=pltpu.CompilerParams(
            collective_id=collective_id, has_side_effects=True, vmem_limit_bytes=52 * 2**20
        ),
    )(*blocks, *operands)
    if joined:
        return sums
    sums, made = sums[:many], sums[many:]
    replica = lax.axis_index("dp")
    core, plane = replica % 2, (replica // 2) % 2
    total = []
    for part in sums:
        side = split_columns(part.shape[1])[0]
        rows = lax.broadcasted_iota(jnp.int32, part.shape, 0)
        kind = lax.broadcasted_iota(jnp.int32, part.shape, 1) // side
        mine = (rows // (part.shape[0] // 2) == core) & ((kind >= 2) | (kind == plane))
        total.append(lax.psum(jnp.where(mine, part, 0).astype(jnp.bfloat16), "dp"))
    return [*total, *made]


def scan_steps(n, reverse, x_ref, y_ref, held, sent, send_sem, recv_sem, out_send, out_recv):
    me, replica = lax.axis_index("seq"), lax.axis_index("dp")
    share = x_ref.shape[0] // n
    width = y_ref.shape[1]

    def span(index):
        return pl.ds(index * share, share)

    def spread(off):
        target = (me + off) % n
        return pltpu.make_async_remote_copy(
            src_ref=x_ref.at[span(target)],
            dst_ref=held.at[me],
            send_sem=send_sem.at[off - 1],
            recv_sem=recv_sem.at[off - 1],
            device_id=(target, replica),
            device_id_type=MESH,
        )

    def arrive(off):
        source = (me + n - off) % n
        return pltpu.make_async_remote_copy(
            src_ref=x_ref.at[span(me)],
            dst_ref=held.at[source],
            send_sem=send_sem.at[off - 1],
            recv_sem=recv_sem.at[off - 1],
            device_id=(source, replica),
            device_id_type=MESH,
        )

    def give(off):
        target = (me + off) % n
        return pltpu.make_async_remote_copy(
            src_ref=sent.at[target],
            dst_ref=y_ref.at[span(me)],
            send_sem=out_send.at[off - 1],
            recv_sem=out_recv.at[off - 1],
            device_id=(target, replica),
            device_id_type=MESH,
        )

    def take(off):
        source = (me + n - off) % n
        return pltpu.make_async_remote_copy(
            src_ref=sent.at[me],
            dst_ref=y_ref.at[span(source)],
            send_sem=out_send.at[off - 1],
            recv_sem=out_recv.at[off - 1],
            device_id=(source, replica),
            device_id_type=MESH,
        )

    def begin():
        for off in range(1, n):
            spread(off).start()
        held[me] = x_ref[span(me)]

    def carry():
        for off in range(1, n):
            arrive(off).wait_recv()
        for p in range(share):
            state = jnp.zeros(y_ref.shape[1:], jnp.float32)
            for s in range(n - 1, -1, -1) if reverse else range(n):
                sent[s, p] = state.astype(sent.dtype)
                passing = held[s, p, width : width + ROWS].astype(jnp.float32)[:1]
                state = passing * state + held[s, p, :width].astype(jnp.float32)
        for off in range(1, n):
            give(off).start()
        y_ref[span(me)] = sent[me]

    def end():
        for off in range(1, n):
            take(off).wait_recv()
        for off in range(1, n):
            spread(off).wait_send()
            give(off).wait_send()

    return (begin, carry, end)


def scan_scratch(pairs, n):
    share = pairs // n
    return [
        pltpu.VMEM((pairs, VH + ROWS, KH), jnp.bfloat16),
        pltpu.VMEM((n, share, VH + ROWS, KH), jnp.bfloat16),
        pltpu.VMEM((n, share, VH, KH), jnp.bfloat16),
        *[pltpu.SemaphoreType.DMA((n - 1,))] * 4,
    ]


def each_head(pairs, span, act):
    def turn(p, carry):
        seq, head = p // HEADS, p % HEADS
        rows = pl.ds(pl.multiple_of(seq * span, span), span)

        def keys(ref):
            return ref.at[rows, pl.ds(pl.multiple_of(head * KH, KH), KH)]

        def values(ref):
            return ref.at[rows, pl.ds(pl.multiple_of(head * VH, VH), VH)]

        def state(ref):
            return ref.at[pl.ds(p, 1)]

        act(keys, values, state)
        return carry

    lax.fori_loop(0, pairs, turn, 0)


def forward_beside(
    n, q, k, v, logits, gate, gain, mixed, gated, running, memory, packed, held, sent, *sems
):
    pairs = packed.shape[0]
    span = q.shape[0] // (pairs // HEADS)
    begin, carry, end = scan_steps(n, False, packed, memory, held, sent, *sems)

    def deposit(keys, values, state):
        deposit_kernel(keys(k), values(v), keys(logits), keys(running), state(packed))

    def mix(keys, values, state):
        mix_kernel(
            keys(q),
            keys(k),
            values(v),
            keys(running),
            state(memory),
            values(gate),
            gain,
            values(mixed),
            values(gated),
        )

    def work(step):
        if step == 0:
            each_head(pairs, span, deposit)
            begin()
        if step == 3:
            carry()
        if step == 5:
            end()
            each_head(pairs, span, mix)

    return work


def backward_beside(
    n,
    grad,
    mixed,
    gate,
    gain,
    q,
    k,
    v,
    running,
    logits,
    memory,
    g_gate,
    g_gain,
    g_q,
    g_k,
    g_v,
    g_logits,
    g_mixed,
    later,
    packed,
    held,
    sent,
    *sems,
):
    pairs = packed.shape[0]
    span = q.shape[0] // (pairs // HEADS)
    begin, carry, end = scan_steps(n, True, packed, later, held, sent, *sems)

    def gate_back(keys, values, state):
        gate_back_kernel(
            values(grad),
            values(mixed),
            values(gate),
            gain,
            keys(q),
            keys(running),
            values(g_gate),
            values(g_mixed),
            g_gain,
            state(packed),
        )

    def span_back(keys, values, state):
        span_back_kernel(
            keys(q),
            keys(k),
            values(v),
            keys(running),
            keys(logits),
            values(g_mixed),
            state(memory),
            state(later),
            keys(g_q),
            keys(g_k),
            values(g_v),
            keys(g_logits),
        )

    def work(step):
        if step == 0:
            g_gain[...] = jnp.zeros_like(g_gain)
            each_head(pairs, span, gate_back)
            begin()
        if step == 3:
            carry()
        if step == 5:
            end()
            each_head(pairs, span, span_back)

    return work


def matmul(left, right):
    return jnp.dot(left, right, preferred_element_type=jnp.float32)


def inner_rows(left, right):
    return lax.dot_general(
        left, right, (((0,), (0,)), ((), ())), preferred_element_type=jnp.float32
    )


def inner_low(left, right):
    return inner_rows(left, right).astype(jnp.bfloat16)


def times_transposed(left, right):
    return lax.dot_general(
        left, right, (((1,), (1,)), ((), ())), preferred_element_type=jnp.float32
    )


def rms_scale(source):
    return lax.rsqrt(jnp.mean(source * source, axis=-1, keepdims=True) + EPS)


def head_scale(source):
    return lax.rsqrt(jnp.maximum(jnp.mean(source * source, axis=-1, keepdims=True), 1.0))


def norm_back(grad_unit, unit, scale):
    return scale * (grad_unit - unit * jnp.mean(grad_unit * unit, axis=-1, keepdims=True))


def head_norm_back(grad_unit, unit, scale):
    live = jnp.where(scale < 1.0, 1.0, 0.0)
    return scale * (grad_unit - live * unit * jnp.mean(grad_unit * unit, axis=-1, keepdims=True))


def low_dot(left, right, left_axis=1, right_axis=0):
    return lax.dot_general(
        left.astype(jnp.bfloat16),
        right.astype(jnp.bfloat16),
        (((left_axis,), (right_axis,)), ((), ())),
        preferred_element_type=jnp.float32,
    )


def exact_sums(ones, source):
    total = jnp.zeros(source.shape, jnp.float32)
    for _ in range(3):
        high = source.astype(jnp.bfloat16)
        total = total + low_dot(ones, high)
        source = source - high.astype(jnp.float32)
    return total


def causal_mask(span):
    target = lax.broadcasted_iota(jnp.int32, (span, span), 0)
    source = lax.broadcasted_iota(jnp.int32, (span, span), 1)
    return target >= source


def pack(packed_ref, state, ending):
    width = state.shape[0]
    packed_ref[0, :width, :] = state.astype(jnp.bfloat16)
    tail = jnp.broadcast_to(jnp.exp(ending), (ROWS, ending.shape[1]))
    packed_ref[0, width:, :] = tail.astype(jnp.bfloat16)


def deposit_kernel(k_ref, v_ref, logits_ref, running_ref, packed_ref):
    logits = logits_ref[...]
    span = logits.shape[0]
    log_decay = (jnp.minimum(logits, 0.0) - jnp.log1p(jnp.exp(-jnp.abs(logits)))) / 16.0
    running = exact_sums(jnp.where(causal_mask(span), 1.0, 0.0), log_decay)
    running_ref[...] = running
    ending = running[span - 1 :, :]
    weighted = jnp.exp(ending - running) * k_ref[...].astype(jnp.float32)
    pack(packed_ref, low_dot(v_ref[...], weighted, 0, 0), ending)


def mix_kernel(q_ref, k_ref, v_ref, running_ref, memory_ref, gate_ref, gain_ref, mixed_ref, gated_ref):
    running = running_ref[...]
    span = running.shape[0]
    middle = running[span // 2 - 1 : span // 2, :]
    queries = q_ref[...].astype(jnp.float32) * KH ** (-0.5)
    rising = queries * jnp.exp(running - middle)
    falling = k_ref[...].astype(jnp.float32) * jnp.exp(middle - running)
    scores = jnp.where(causal_mask(span), low_dot(rising, falling, 1, 1), 0.0)
    mixed = low_dot(scores, v_ref[...])
    mixed = mixed + low_dot(queries * jnp.exp(running), memory_ref[0], 1, 1)
    mixed_ref[...] = mixed
    normed = mixed * head_scale(mixed) * gain_ref[...]
    gate = gate_ref[...]
    gated_ref[...] = (normed * gate * jax.nn.sigmoid(gate)).astype(jnp.bfloat16)


def gate_back_kernel(
    grad_ref, mixed_ref, gate_ref, gain_ref, q_ref, running_ref, gate_out_ref, g_ref, gain_out_ref, packed_ref
):
    grad, mixed, gate, gain = grad_ref[...], mixed_ref[...], gate_ref[...], gain_ref[...]
    scale = head_scale(mixed)
    unit = mixed * scale
    sig = jax.nn.sigmoid(gate)
    slope = sig * (1.0 + gate * (1.0 - sig))
    gate_out_ref[...] = (grad * unit * gain * slope).astype(jnp.bfloat16)
    grad_heads = grad * gate * sig

    gain_out_ref[...] += jnp.sum(grad_heads * unit, axis=0, keepdims=True)
    g_mixed = head_norm_back(grad_heads * gain, unit, scale).astype(jnp.bfloat16)
    g_ref[...] = g_mixed
    running = running_ref[...]
    span = running.shape[0]
    grown = q_ref[...].astype(jnp.float32) * KH ** (-0.5) * jnp.exp(running)
    pack(packed_ref, low_dot(g_mixed, grown, 0, 0), running[span - 1 :, :])


def span_back_kernel(
    q_ref, k_ref, v_ref, running_ref, logits_ref, g_ref, memory_ref, later_ref, gq_ref, gk_ref, gv_ref, gl_ref
):
    running, g, memory, later = running_ref[...], g_ref[...], memory_ref[0], later_ref[0]
    values = v_ref[...]
    span = running.shape[0]
    middle = running[span // 2 - 1 : span // 2, :]
    ending = running[span - 1 :, :]
    queries = q_ref[...].astype(jnp.float32) * KH ** (-0.5)
    key_rows = k_ref[...].astype(jnp.float32)
    grow, shrink = jnp.exp(running - middle), jnp.exp(middle - running)
    start, left = jnp.exp(running), jnp.exp(ending - running)
    rising = (queries * grow).astype(jnp.bfloat16)
    falling = (key_rows * shrink).astype(jnp.bfloat16)
    entered = (queries * start).astype(jnp.bfloat16)
    carried = (key_rows * left).astype(jnp.bfloat16)
    causal = causal_mask(span)
    scores = jnp.where(causal, low_dot(rising, falling, 1, 1), 0.0)
    g_scores = jnp.where(causal, low_dot(g, values, 1, 1), 0.0).astype(jnp.bfloat16)
    dq_within = low_dot(g_scores, falling)
    dk_within = low_dot(g_scores, rising, 0, 0)
    dq_across = low_dot(g, memory)
    dk_across = low_dot(values, later)
    gq_ref[...] = (KH ** (-0.5) * (grow * dq_within + start * dq_across)).astype(jnp.bfloat16)
    gk_ref[...] = (shrink * dk_within + left * dk_across).astype(jnp.bfloat16)
    gv_ref[...] = (low_dot(scores, g, 0, 0) + low_dot(carried, later, 1, 1)).astype(jnp.bfloat16)
    leaving = carried.astype(jnp.float32) * dk_across
    change = rising.astype(jnp.float32) * dq_within + entered.astype(jnp.float32) * dq_across
    change = change - falling.astype(jnp.float32) * dk_within - leaving
    kept = jnp.sum(memory.astype(jnp.float32) * later.astype(jnp.float32), axis=0, keepdims=True)
    at_end = jnp.sum(leaving, axis=0, keepdims=True) + jnp.exp(ending) * kept
    target = lax.broadcasted_iota(jnp.int32, (span, span), 0)
    source = lax.broadcasted_iota(jnp.int32, (span, span), 1)
    g_decay = exact_sums(jnp.where(source >= target, 1.0, 0.0), change) + at_end
    gl_ref[...] = g_decay * jax.nn.sigmoid(-logits_ref[...]) / 16.0


def forward(whole, inputs, ff_shards):
    (
        attn_gain,
        w_query,
        w_key,
        w_value,
        w_gate,
        w_rank_in,
        w_rank_out,
        rank_bias,
        out_gain,
        w_out,
        mlp_gain,
    ) = whole
    seqs, span, width = inputs.shape
    count = seqs * span
    rows_in = inputs.astype(jnp.float32).reshape(count, width)
    scale_in = rms_scale(rows_in)
    unit_in = rows_in * scale_in
    normed_in = (unit_in * attn_gain.astype(jnp.float32)).astype(jnp.bfloat16)
    queries = matmul(normed_in, w_query).astype(jnp.bfloat16)
    key_rows = matmul(normed_in, w_key).astype(jnp.bfloat16)
    values = matmul(normed_in, w_value).astype(jnp.bfloat16)
    gate_out = matmul(normed_in, w_gate)
    rank_rows = matmul(normed_in, w_rank_in)
    logits = jnp.dot(rank_rows, w_rank_out.astype(jnp.float32), precision=HIGH) + rank_bias.astype(
        jnp.float32
    )
    n = lax.axis_size("seq")
    pairs = seqs * HEADS
    up_pair, w_down, mixed, gated, running, memory_in = gather_all(
        ff_shards,
        1,
        forward_beside,
        (
            queries,
            key_rows,
            values,
            logits,
            gate_out,
            out_gain.astype(jnp.float32).reshape(1, VH),
        ),
        (
            jax.ShapeDtypeStruct((count, HEADS * VH), jnp.float32),
            jax.ShapeDtypeStruct((count, HEADS * VH), jnp.bfloat16),
            jax.ShapeDtypeStruct((count, HEADS * KH), jnp.float32),
            jax.ShapeDtypeStruct((pairs, VH, KH), jnp.bfloat16),
        ),
        scan_scratch(pairs, n),
    )
    hidden_width = up_pair.shape[1] // 2
    w_gate_ff, w_up = up_pair[:, :hidden_width], up_pair[:, hidden_width:]
    middle = rows_in + matmul(gated, w_out)
    scale_mid = rms_scale(middle)
    unit_mid = middle * scale_mid
    normed_mid = (unit_mid * mlp_gain.astype(jnp.float32)).astype(jnp.bfloat16)
    gate_ff = matmul(normed_mid, w_gate_ff)
    up_rows = matmul(normed_mid, w_up)
    hidden = (jax.nn.silu(gate_ff) * up_rows).astype(jnp.bfloat16)
    output = (middle + matmul(hidden, w_down)).astype(jnp.bfloat16).reshape(seqs, span, width)
    return (
        unit_in,
        scale_in,
        normed_in,
        queries,
        key_rows,
        values,
        running,
        memory_in,
        gate_out,
        rank_rows,
        logits,
        mixed,
        gated,
        unit_mid,
        scale_mid,
        normed_mid,
        gate_ff,
        up_rows,
        hidden,
        output,
        w_gate_ff,
        w_up,
        w_down,
    )


def backward(whole, kept, cotangent):
    (
        attn_gain,
        w_query,
        w_key,
        w_value,
        w_gate,
        w_rank_in,
        w_rank_out,
        rank_bias,
        out_gain,
        w_out,
        mlp_gain,
    ) = whole
    (
        unit_in,
        scale_in,
        normed_in,
        queries,
        key_rows,
        values,
        running,
        memory_in,
        gate_out,
        rank_rows,
        logits,
        mixed,
        gated,
        unit_mid,
        scale_mid,
        normed_mid,
        gate_ff,
        up_rows,
        hidden,
        output,
        w_gate_ff,
        w_up,
        w_down,
    ) = kept
    seqs, span, width = cotangent.shape
    count = seqs * span
    grad_rows = cotangent.reshape(count, width)
    grad_down = inner_low(hidden, grad_rows)
    grad_hidden = times_transposed(grad_rows, w_down)
    sig_ff = jax.nn.sigmoid(gate_ff)
    slope_ff = sig_ff * (1.0 + gate_ff * (1.0 - sig_ff))
    grad_gate_ff = (grad_hidden * up_rows * slope_ff).astype(jnp.bfloat16)
    grad_up_rows = (grad_hidden * gate_ff * sig_ff).astype(jnp.bfloat16)
    grad_pair_w = inner_low(normed_mid, jnp.concatenate([grad_gate_ff, grad_up_rows], axis=1))
    grad_normed_mid = times_transposed(grad_gate_ff, w_gate_ff) + times_transposed(
        grad_up_rows, w_up
    )
    grad_mlp_gain = jnp.sum(grad_normed_mid * unit_mid, axis=0)
    grad_middle = grad_rows.astype(jnp.float32) + norm_back(
        grad_normed_mid * mlp_gain.astype(jnp.float32), unit_mid, scale_mid
    )
    grad_branch = grad_middle.astype(jnp.bfloat16)
    grad_out_w = inner_low(gated, grad_branch)
    grad_gated = times_transposed(grad_branch, w_out)
    pairs = seqs * HEADS
    keys, vals = (count, HEADS * KH), (count, HEADS * VH)
    (
        grad_pair_w,
        grad_down,
        grad_gate_out,
        grad_out_gain,
        grad_queries,
        grad_keys,
        grad_values,
        grad_logits,
    ) = reduce_all(
        [grad_pair_w, grad_down],
        2,
        backward_beside,
        (
            grad_gated,
            mixed,
            gate_out,
            out_gain.astype(jnp.float32).reshape(1, VH),
            queries,
            key_rows,
            values,
            running,
            logits,
            memory_in,
        ),
        (
            jax.ShapeDtypeStruct(vals, jnp.bfloat16),
            jax.ShapeDtypeStruct((1, VH), jnp.float32),
            jax.ShapeDtypeStruct(keys, jnp.bfloat16),
            jax.ShapeDtypeStruct(keys, jnp.bfloat16),
            jax.ShapeDtypeStruct(vals, jnp.bfloat16),
            jax.ShapeDtypeStruct(keys, jnp.float32),
        ),
        (
            pltpu.VMEM(vals, jnp.bfloat16),
            pltpu.VMEM((pairs, VH, KH), jnp.bfloat16),
            *scan_scratch(pairs, lax.axis_size("seq")),
        ),
    )
    grad_bias = jnp.sum(grad_logits, axis=0)
    grad_rank_out = jnp.einsum("rq,rk->qk", rank_rows, grad_logits, precision=HIGH)
    grad_rank_rows = jnp.einsum(
        "rk,qk->rq", grad_logits, w_rank_out.astype(jnp.float32), precision=HIGH
    )
    grad_rank_in = jnp.einsum(
        "rd,rq->dq", normed_in.astype(jnp.float32), grad_rank_rows, precision=HIGH
    )
    grad_mixer_w = inner_low(
        normed_in, jnp.concatenate([grad_queries, grad_keys, grad_values, grad_gate_out], axis=1)
    )
    grad_normed_in = times_transposed(grad_queries, w_query) + times_transposed(grad_keys, w_key)
    grad_normed_in = (
        grad_normed_in
        + times_transposed(grad_values, w_value)
        + times_transposed(grad_gate_out, w_gate)
    )
    grad_normed_in = grad_normed_in + jnp.einsum(
        "rq,dq->rd", grad_rank_rows, w_rank_in.astype(jnp.float32), precision=HIGH
    )
    grad_attn_gain = jnp.sum(grad_normed_in * unit_in, axis=0)
    input_grad = grad_middle + norm_back(
        grad_normed_in * attn_gain.astype(jnp.float32), unit_in, scale_in
    )
    grads = (
        (grad_attn_gain, grad_rank_out, grad_bias, grad_out_gain, grad_mlp_gain),
        grad_mixer_w,
        grad_out_w,
        grad_rank_in,
        grad_pair_w,
        grad_down,
    )
    return (grads, input_grad.astype(jnp.bfloat16).reshape(seqs, span, width))


def body(
    inputs,
    cotangent,
    attn_gain,
    w_query,
    w_key,
    w_value,
    w_gate,
    w_rank_in,
    w_rank_out,
    rank_bias,
    out_gain,
    w_out,
    mlp_gain,
    w_gate_ff,
    w_up,
    w_down,
):
    n = lax.axis_size("seq")
    gains = (attn_gain, w_rank_out, rank_bias, out_gain, mlp_gain)
    rows = w_query.shape[0]
    flat = jnp.concatenate([gain.reshape(-1) for gain in gains])
    flat = jnp.pad(flat, (0, rows * SMALL - flat.size)).reshape(rows, SMALL)
    spare = jnp.zeros((rows, 128 - w_rank_in.shape[1] - SMALL), w_query.dtype)
    tail = jnp.concatenate([w_rank_in, flat, spare], axis=1)
    (mixer,) = gather_all([[w_query, w_key, w_value, w_gate, w_out, tail]], 0)
    cuts = [0]
    for weight in (w_query, w_key, w_value, w_gate, w_out, w_rank_in):
        cuts.append(cuts[-1] + weight.shape[1])
    parts = [mixer[:, low:high] for low, high in zip(cuts[:-1], cuts[1:])]
    flat = mixer[:, cuts[-1] : cuts[-1] + SMALL].reshape(n, rows * SMALL)
    small, at = [], 0
    for gain in gains:
        piece = flat[:, at : at + gain.size].reshape(n * gain.shape[0], *gain.shape[1:])
        small.append(piece)
        at += gain.size
    whole = (
        small[0],
        parts[0],
        parts[1],
        parts[2],
        parts[3],
        parts[5],
        small[1],
        small[2],
        small[3],
        parts[4],
        small[4],
    )
    kept = forward(whole, inputs, [[w_gate_ff, w_up], [w_down]])
    output = kept[-4]
    grads, input_grad = backward(whole, kept, cotangent)
    gain_grads, mixer, grad_out_w, grad_rank_in, up_pair, down = grads
    flat = jnp.concatenate(
        [grad.astype(jnp.bfloat16).reshape(n, -1) for grad in gain_grads], axis=1
    )
    flat = jnp.pad(flat, ((0, 0), (0, rows * SMALL - flat.shape[1]))).reshape(n * rows, SMALL)
    spare = jnp.zeros((n * rows, spare.shape[1]), jnp.bfloat16)
    rest = jnp.concatenate(
        [grad_out_w, grad_rank_in.astype(jnp.bfloat16), flat, spare], axis=1
    )
    mixer, rest = reduce_all([mixer, rest], 3)
    mixer = jnp.concatenate([mixer, rest], axis=1).astype(jnp.float32)
    up_pair = up_pair.astype(jnp.float32)
    parts = [mixer[:, start:end] for start, end in zip(cuts[:-1], cuts[1:])]
    flat = mixer[:, cuts[-1] : cuts[-1] + SMALL].reshape(-1)
    small, at = [], 0
    for gain in gains:
        small.append(flat[at : at + gain.size].reshape(gain.shape))
        at += gain.size
    summed = (
        small[0],
        parts[0],
        parts[1],
        parts[2],
        parts[3],
        parts[5],
        small[1],
        small[2],
        small[3],
        parts[4],
        small[4],
        up_pair[:, : w_gate_ff.shape[1]],
        up_pair[:, w_gate_ff.shape[1] :],
        down.astype(jnp.float32),
    )
    return (
        output,
        input_grad,
        summed[0],
        summed[1],
        summed[2],
        summed[3],
        summed[4],
        summed[5],
        summed[6],
        summed[7],
        summed[8],
        summed[9],
        summed[10],
        summed[11],
        summed[12],
        summed[13],
    )


def solution(mesh):
    placed = (
        P("dp", "seq", None),
        P("dp", "seq", None),
        P("seq"),
        P("seq", None),
        P("seq", None),
        P("seq", None),
        P("seq", None),
        P("seq", None),
        P("seq", None),
        P("seq"),
        P("seq"),
        P("seq", None),
        P("seq"),
        P("seq", None),
        P("seq", None),
        P("seq", None),
    )
    return jax.shard_map(
        body,
        mesh=mesh,
        in_specs=placed,
        out_specs=(
            P("dp", "seq", None),
            P("dp", "seq", None),
            P("seq"),
            P("seq", None),
            P("seq", None),
            P("seq", None),
            P("seq", None),
            P("seq", None),
            P("seq", None),
            P("seq"),
            P("seq"),
            P("seq", None),
            P("seq"),
            P("seq", None),
            P("seq", None),
            P("seq", None),
        ),
        check_vma=False,
    )
```

time: 664 us -> 412 us (0.62); the launches traced: 653 us -> 411 us
  Pallas kernels: 425 us -> 314 us
  local copies, waits for them, and re-layouts: 86.4 us -> 26.8 us
  matrix products: 107 us -> 63.4 us
  other arithmetic: 32.1 us -> 5.28 us
    pallas_call x4, Pallas kernels: 425 us -> 314 us  [the longest x2 168 us: reduce_all(): pl.pallas_call(functools.partial(reduce_kernel, n, many, joined, beside,...]
    dot_general x30 -> x0, matrix products: 39.4 us -> none  [the longest x8 14.5 us: block_step(): deposit = jnp.einsum('bhsk,bhsv->bhkv', carried, values, precision=HIGH)]
    squeeze x14 -> x0, local copies, waits for them, and re-layouts: 14.1 us -> none  [span_attention(): lax.scan(jax.checkpoint(block_step), memory_in, pieces)]
    concatenate x4, local copies, waits for them, and re-layouts: 17 us -> 3.99 us  [the longest x2 3.82 us: body(): jnp.concatenate([grad_out_w, grad_rank_in.astype(jnp.bfloat16), flat, spa...]
    another operation x10 -> x0, local copies, waits for them, and re-layouts: 11.6 us -> none  [the longest x4 7.91 us: to_blocks(): blocked = source.reshape(seqs, span // BLOCK, BLOCK, HEADS, width)]
    concatenate x4 -> x1, other arithmetic: 9.87 us -> 0.09 us  [body(): tail = jnp.concatenate([w_rank_in, flat, spare], axis=1)]
    transpose x6 -> x0, local copies, waits for them, and re-layouts: 9.67 us -> none  [the longest x4 7.59 us: to_blocks(): return blocked.transpose(1, 0, 3, 2, 4)]
    another operation x12 -> x0, other arithmetic: 8.48 us -> none  [the longest x10 8.34 us: block_step(): running = jnp.cumsum(log_decay, axis=2)]
where the time goes in v2:
time: 412 us; the launch traced here: 411 us
  Pallas kernels  314 us (76%)
  matrix products  63.4 us (15%)
  local copies, waits for them, and re-layouts  26.8 us (7%)
  other arithmetic  5.28 us (1%)
    pallas_call x2, Pallas kernels, reduce_all(): pl.pallas_call(functools.partial(reduce_kernel, n, many, joined, beside,...  168 us
    pallas_call x2, Pallas kernels, gather_all(): pl.pallas_call(functools.partial(gather_kernel, n, many, tuple(layout), b...  146 us
    dot_general x9, matrix products, matmul(): return jnp.dot(left, right, preferred_element_type=jnp.float32)  24.3 us
    dot_general x8, matrix products, times_transposed(): lax.dot_general(left, right, (((1,), (1,)), ((), ())), preferred_element_...  19.5 us
    dot_general x4, matrix products, inner_rows(): lax.dot_general(left, right, (((0,), (0,)), ((), ())), preferred_element_...  15.5 us
    unnamed x53, local copies, waits for them, and re-layouts  9.29 us

profile of v2, /device:TPU:0, one launch (start us, length us, event | category | flops | bytes accessed | tf_op | source)
XLA Modules:
  0.0 410.6 jit_solution(1122826754099035426)
XLA Ops:
  1.3 2.8 concatenate.28
  9.8 49.7 %shard_map.279 = bf16[8,128,4224]{2,1,0:T(8,128)(2,1)} custom-call(bf16[128,512]{1,0:T(8,128)(2,1)S(1)} %copy-done.10, bf16[128,512]{1,0:T(8,128)(2,1)S(1)} %copy-done.11, bf16[128,1024]{1,0:T(8,128)(2,1)S(1)} %copy-done.7, bf16[128,1024]{1,0:T(8,128)(2,1)S(1)} %copy-done.8, bf16[128,1024]{1,0:T(8,128)(2,1)S(1)} %copy-done.9, ...), custom_call_target="tpu_custom_call" | custom-call | tf_op jit(solution)/shard_map/pallas_call | solution.py:204
  61.4 1.9 convolution_convert_fusion.5.refs_3_.refs_6_
  64.9 2.3 fusion.39.refs_5_.refs_8_
  67.3 2.0 fusion.50
  71.8 3.6 fusion.17.refs_7_.refs_4_
  78.6 96.8 %shard_map.280 = (bf16[8,128,5632]{2,1,0:T(8,128)(2,1)}, bf16[8,352,1024]{2,1,0:T(8,128)(2,1)}, f32[256,1024]{1,0:T(8,128)}, bf16[256,1024]{1,0:T(8,128)(2,1)S(1...) custom-call(bf16[128,2816]{1,0:T(8,128)(2,1)S(1)} %copy-done.2, bf16[128,2816]{1,0:T(8,128)(2,1)S(1)} %copy-done.3, ...), custom_call_target="tpu_custom_call" | custom-call | tf_op jit(solution)/shard_map/pallas_call | solution.py:204
  175.5 2.8 multiply_reduce_fusion.4
  178.3 4.5 %convolution_bitcast_fusion = f32[256,2816]{1,0:T(8,128)S(1)} fusion(bf16[2816,1024]{1,0:T(8,128)(2,1)} %bitcast.107, bf16[256,1024]{1,0:T(8,128)(2,1)S(1)} %bitcast.95), kind=kOutput, calls=%fused_computation.11 | convolution fusion | flops 1476395008 | bytes 9175040 | tf_op jit(solution)/shard_map/dot_general | solution.py:740
  185.9 3.3 multiply_convert_fusion.1
  189.2 5.1 %fusion.38 = bf16[256,1024]{1,0:T(8,128)(2,1)} fusion(f32[256,1024]{1,0:T(8,128)S(1)} %get-tuple-element.99, bf16[256,2816]{1,0:T(8,128)(2,1)S(1)} %get-tuple-element.85, bf16[2816,1024]{1,0:T(8,128)(2,1)} %bitcast.108), kind=kOutput, calls=%fused_computation.46 | convolution fusion | flops 1476919296 | bytes 8781824 | tf_op jit(solution)/shard_map/dot_general | solution.py:726
  196.0 1.8 multiply_reduce_fusion
  198.2 6.0 %convolution_convert_fusion = bf16[1024,5632]{1,0:T(8,128)(2,1)} fusion(bf16[256,1024]{1,0:T(8,128)(2,1)S(1)} %multiply_convert_fusion.3, bf16[256,2816]{1,0:T(8,128)(2,1)S(1)} %get-tuple-element.86, bf16[256,2816]{1,0:T(8,128)(2,1)S(1)} %get-tuple-element.84), kind=kOutput, calls=%fused_computation | convolution fusion | flops 2964324352 | bytes 14942208 | tf_op jit(solution)/shard_map/dot_general | solution.py:730
  204.2 4.2 %convolution_convert_fusion.2 = bf16[2816,1024]{1,0:T(8,128)(2,1)} fusion(bf16[256,2816]{1,0:T(8,128)(2,1)S(1)} %get-tuple-element.85, bf16[256,1024]{1,0:T(8,128)(2,1)S(1)} %bitcast.96), kind=kOutput, calls=%fused_computation.2 | convolution fusion | flops 1479278592 | bytes 7733248 | tf_op jit(solution)/shard_map/dot_general | solution.py:730
  208.4 3.3 fusion.11.refs_2_
  211.7 108.2 %shard_map.281 = (bf16[128,5632]{1,0:T(8,128)(2,1)}, bf16[352,1024]{1,0:T(8,128)(2,1)}, bf16[256,1024]{1,0:T(8,128)(2,1)S(1)}, f32[1,256]{1,0:T(1,128)S(1)}, bf1...) custom-call(bf16[8,128,5632]{2,1,0:T(8,128)(2,1)} %bitcast.77, ...), custom_call_target="tpu_custom_call" | custom-call | tf_op jit(solution)/shard_map/pallas_call | solution.py:457
  320.0 2.4 fusion.15
  322.4 2.3 fusion.19
  326.5 1.8 fusion.31
  328.6 2.0 multiply_reduce_fusion.1
  331.7 4.5 %convolution_convert_fusion.1 = bf16[1024,3072]{1,0:T(8,128)(2,1)} fusion(bf16[256,1024]{1,0:T(8,128)(2,1)S(1)} %copy-done.15, bf16[256,1024]{1,0:T(8,128)(2,1)S(1)} %get-tuple-element.41, bf16[256,1024]{1,0:T(8,128)(2,1)S(1)} %copy-done.24, bf16[256,512]{1,0:T(8,128)(2,1)S(1)} %get-tuple-element.39, bf16[256,512]{1,0:T(8,128)(2,1)S(1)} %get-tuple-element.38), kind=kOutput, calls=%fused_computation.1 | convolution fusion | flops 1620049920 | bytes 8388608 | tf_op jit(solution)/shard_map/dot_general | solution.py:730
  338.5 3.6 concatenate.36.refs_1_
  342.1 59.3 %shard_map.282 = (bf16[128,3072]{1,0:T(8,128)(2,1)S(1)}, bf16[128,1152]{1,0:T(8,128)(2,1)S(1)}) custom-call(bf16[8,128,3072]{2,1,0:T(8,128)(2,1)} %bitcast.94, bf16[8,128,1152]{2,1,0:T(8,128)(2,1)} %concatenate.36.refs_1_), custom_call_target="tpu_custom_call" | custom-call | tf_op jit(solution)/shard_map/pallas_call | solution.py:457
  407.6 1.8 fusion.58
  (109 shorter events, 33.6 us)
Async XLA Ops:
  5.2 1.0 copy-start.7
  6.1 0.9 copy-start.8
  7.1 0.9 copy-start.9
  8.0 0.9 copy-start.10
  9.8 51.2 %copy-start.12 = (bf16[2,128,1024]{2,1,0:T(8,128)(2,1)S(1)}, bf16[2,128,1024]{2,1,0:T(8,128)(2,1)}, u32[]{:S(2)}) copy-start(bf16[2,128,1024]{2,1,0:T(8,128)(2,1)} %param.16) | copy-start | bytes 1572868
  60.9 9.0 %copy-start.22 = (bf16[8,2048]{1,0:T(8,128)(2,1)}, bf16[8,2048]{1,0:T(8,128)(2,1)S(1)}, u32[]{:S(2)}) copy-start(bf16[8,2048]{1,0:T(8,128)(2,1)S(1)} %reshape.182) | copy-start | bytes 98308
  61.4 5.9 %copy-start.14 = (bf16[256,1024]{1,0:T(8,128)(2,1)}, bf16[256,1024]{1,0:T(8,128)(2,1)S(1)}, u32[]{:S(2)}) copy-start(bf16[256,1024]{1,0:T(8,128)(2,1)S(1)} %multiply_convert_fusion.4) | copy-start | bytes 1572868
  67.3 108.2 %copy-start.1 = (bf16[256,1024]{1,0:T(8,128)(2,1)}, bf16[256,1024]{1,0:T(8,128)(2,1)S(1)}, u32[]{:S(2)}) copy-start(bf16[256,1024]{1,0:T(8,128)(2,1)S(1)} %fusion.39.refs_5_.refs_8_) | copy-start | bytes 1572868
  67.3 10.2 %copy-start.2 = (bf16[128,2816]{1,0:T(8,128)(2,1)S(1)}, bf16[128,2816]{1,0:T(8,128)(2,1)}, u32[]{:S(2)}) copy-start(bf16[128,2816]{1,0:T(8,128)(2,1)} %refs_0_.3) | copy-start | bytes 2162692
  67.3 10.2 %copy-start.3 = (bf16[128,2816]{1,0:T(8,128)(2,1)S(1)}, bf16[128,2816]{1,0:T(8,128)(2,1)}, u32[]{:S(2)}) copy-start(bf16[128,2816]{1,0:T(8,128)(2,1)} %refs_1_.3) | copy-start | bytes 2162692
  71.8 103.7 %copy-start = (f32[256,512]{1,0:T(8,128)}, f32[256,512]{1,0:T(8,128)S(1)}, u32[]{:S(2)}) copy-start(f32[256,512]{1,0:T(8,128)S(1)} %convolution_add_fusion.3.refs_6_.refs_10_) | copy-start | bytes 1572868
  77.5 1.1 copy-start.4
  175.5 7.3 %copy-start.5 = (f32[256,512]{1,0:T(8,128)}, f32[256,512]{1,0:T(8,128)S(1)}, u32[]{:S(2)}) copy-start(f32[256,512]{1,0:T(8,128)S(1)} %get-tuple-element.36.refs_9_) | copy-start | bytes 1572868
  175.5 7.3 %copy-start.6 = (bf16[8,256,128]{2,1,0:T(8,128)(2,1)}, bf16[8,256,128]{2,1,0:T(8,128)(2,1)S(1)}, u32[]{:S(2)}) copy-start(bf16[8,256,128]{2,1,0:T(8,128)(2,1)S(1)} %get-tuple-element.37.refs_11_) | copy-start | bytes 1572868
  175.5 2.8 copy-start.18
  178.3 6.0 %copy-start.23 = (bf16[8,128,5632]{2,1,0:T(8,128)(2,1)S(1)}, bf16[8,128,5632]{2,1,0:T(8,128)(2,1)}, u32[]{:S(2)}) copy-start(bf16[8,128,5632]{2,1,0:T(8,128)(2,1)} %get-tuple-element.33) | copy-start | bytes 34603012
  320.0 2.4 copy-start.24
  326.4 1.8 copy-start.16
  326.5 1.8 copy-start.21
  328.6 3.1 copy-start.15
  336.2 1.3 copy-start.17
  336.2 1.3 copy-start.20
  404.2 3.4 copy-start.13
  407.6 1.8 copy-start.19
  (1 other events, 0.9 us)
